TPU v7x, 256 devices: a whole 4x4x8 slice. The times are simulated.
256 devices in a mesh: grp: 8 (over y, core), dev: 32 (over z, x).
Axes of the slice: x: 4, y: 4, z: 8, core: 2. Of those that a mesh axis runs over, the one named last changes fastest.
Arguments:
- multipoles: bfloat16 [9, 32, 65536], P(None, None, ('grp', 'dev')), may hold values from -6 to 6
- harmonics: bfloat16 [121, 32, 65536], P(None, None, ('grp', 'dev')), may hold values from -6 to 6
- positions: float32 [3, 32, 65536], P(None, None, ('grp', 'dev')), may hold values from -3 to 3
- atom_counts: int32 [65536], P(('grp', 'dev')), may hold values from 16 to 32
- source_ops: float32 [9, 121, 121], replicated, may hold values from -0.1875 to 0.1875
- field_ops: float32 [9, 121, 121], replicated, may hold values from -0.5 to 0.5
- m2l_ops: bfloat16 [316, 121, 121], replicated, may hold values from -0.03125 to 0.03125
- send_list: int32 [256, 256, 4], P(('grp', 'dev')), may hold values from -1 to 255, as said below
- m2l_list: int32 [316, 65536], P(None, ('grp', 'dev')), may hold values from -1 to 1279, as said below
- near_list: int32 [27, 65536], P(None, ('grp', 'dev')), may hold values from -1 to 287, as said below
Outputs:
- fields: float32 [9, 32, 65536], P(None, None, ('grp', 'dev'))
Inputs may be any that keep to these rules, and one draw needn't show every extreme that they name: `send_list`: -1 marks an unused slot; otherwise a local leaf index of the sending device. `m2l_list`: -1 marks an offset without source; otherwise a column of the device's pool. `near_list`: -1 marks an empty entry; entry 0 is the leaf itself.
All inputs are finite; a program needn't handle non-finite values.
Results may differ from a plain program's by a relative error of at most 0.004.
Values may be sent and summed in bfloat16 or wider, within the bound.
No kernel may reach another device: no remote copies, remote signals or barrier semaphores. Data moves between devices by JAX's collectives and lax.ppermute only.
A program may use at most 128 MiB of HBM per device.

v0:
```python
import jax
import jax.numpy as jnp
from jax import lax
from jax.sharding import PartitionSpec as P

HALO = 16


softening = 0.25


def padded(value, sides, width):
    for axis, dim in sides:
        count, length = (lax.axis_size(axis), value.shape[dim])
        up = [(i, (i + 1) % count) for i in range(count - 1)]
        down = [(j, i) for i, j in up]
        last = lax.slice_in_dim(value, length - width, length, axis=dim)
        initial = lax.slice_in_dim(value, 0, width, axis=dim)
        before = lax.ppermute(last, axis, up)
        after = lax.ppermute(initial, axis, down)
        value = jnp.concatenate([before, value, after], axis=dim)
    return value


def near_field(own_src, extended, near_rows):

    def one_slot(running, slot_row):
        usable = slot_row >= 0
        picked = jnp.take(extended, jnp.clip(slot_row, 0, extended.shape[2] - 1), axis=2)
        picked = jnp.where(usable[None, None, :], picked, 0.0)
        offsets = own_src[:3, :, None, :] - picked[:3, None, :, :]
        inverse = 1.0 / jnp.sqrt(jnp.sum(offsets * offsets, axis=0) + softening)
        inverse_cube = inverse * inverse * inverse
        inverse_five = inverse_cube * inverse * inverse
        charge = picked[3][None, :, :]
        weighted = charge * inverse_cube
        steep_part = 3.0 * charge * inverse_five
        along_x, along_y, along_z = (offsets[0], offsets[1], offsets[2])
        pair_terms = jnp.stack(
            [
                charge * inverse,
                weighted * along_x,
                weighted * along_y,
                weighted * along_z,
                weighted - steep_part * along_x * along_x,
                weighted - steep_part * along_y * along_y,
                -steep_part * along_x * along_y,
                -steep_part * along_x * along_z,
                -steep_part * along_y * along_z,
            ]
        )
        return (running + jnp.sum(pair_terms, axis=2), None)

    initial = jnp.zeros((9, own_src.shape[1], own_src.shape[2]), jnp.float32)
    result, unused = lax.scan(one_slot, initial, near_rows)
    return result


def shards(
    multipoles,
    harmonics,
    positions,
    atom_counts,
    source_ops,
    field_ops,
    m2l_ops,
    send_list,
    m2l_list,
    near_list,
):
    slot_ids = lax.broadcasted_iota(jnp.int32, positions.shape[1:], 0)
    present = slot_ids < atom_counts[None, :]
    masked = jnp.where(present[None], multipoles, jnp.zeros_like(multipoles))
    own_src = jnp.concatenate([positions, masked[0:1].astype(jnp.float32)], axis=0)
    extended = padded(own_src, ((("grp", "dev"), 2),), HALO)
    sources = jnp.einsum("cal,kal->ckl", masked, harmonics, preferred_element_type=jnp.float32)
    moments = jnp.einsum(
        "ckj,ckl->jl", source_ops, sources, precision=lax.Precision.HIGHEST
    ).astype(jnp.bfloat16)
    coef_count = moments.shape[0]
    send_rows = send_list[0]
    slot_count = send_rows.shape[1]
    peer_count = lax.axis_size(("grp", "dev"))
    flat_rows = send_rows.reshape(-1)
    outgoing = jnp.take(moments, jnp.clip(flat_rows, 0, None), axis=1)
    outgoing = jnp.where(flat_rows[None, :] >= 0, outgoing, jnp.zeros_like(outgoing))
    outgoing = outgoing.T.reshape(peer_count, slot_count, coef_count)
    groups = lax.axis_size("grp")
    sectioned = outgoing.reshape(groups, peer_count // groups, slot_count, coef_count)
    arrived = lax.all_to_all(
        lax.all_to_all(sectioned, "grp", split_axis=0, concat_axis=0, tiled=True),
        "dev",
        split_axis=1,
        concat_axis=1,
        tiled=True,
    )
    incoming = arrived.reshape(peer_count, slot_count, coef_count)
    source_pool = jnp.concatenate([moments, incoming.reshape(-1, coef_count).T], axis=1)
    gathered = jnp.take(source_pool, jnp.clip(m2l_list, 0, source_pool.shape[1] - 1), axis=1)
    gathered = jnp.where(m2l_list[None] >= 0, gathered, jnp.zeros_like(gathered))
    local_exp = jnp.einsum("kol,okj->jl", gathered, m2l_ops, preferred_element_type=jnp.float32)
    derived = jnp.einsum(
        "ckj,jl->ckl", field_ops, local_exp, precision=lax.Precision.HIGHEST
    ).astype(jnp.bfloat16)
    far_part = jnp.einsum("ckl,kal->cal", derived, harmonics, preferred_element_type=jnp.float32)
    near_part = near_field(own_src, extended, near_list)
    return jnp.where(present[None], far_part + near_part, 0.0)


def solution(mesh):
    placed = (
        P(None, None, ("grp", "dev")),
        P(None, None, ("grp", "dev")),
        P(None, None, ("grp", "dev")),
        P(("grp", "dev")),
        P(),
        P(),
        P(),
        P(("grp", "dev"), None, None),
        P(None, ("grp", "dev")),
        P(None, ("grp", "dev")),
    )
    return jax.shard_map(
        shards, mesh=mesh, in_specs=placed, out_specs=P(None, None, ("grp", "dev")), check_vma=False
    )
```

profile of v0, /device:TPU:1, one launch (start us, length us, event | category | flops | bytes accessed | tf_op | source)
XLA Modules:
  0.0 1258.2 jit_solution(2716995832555786156)
XLA Ops:
  5.5 11.1 collective-permute-start.1
  19.9 4.3 copy.67
  24.2 4.0 convolution_bitcast_fusion
  29.2 3.1 fusion.26
  32.2 3.2 gather_fusion.1
  36.5 4.6 all-to-all-start
  43.3 4.3 all-to-all-done
  48.4 7.4 all-to-all-start.1
  55.8 851.7 %while.11 = (s32[]{:T(128)}, f32[9,32,256]{2,1,0:T(8,128)S(1)}, f32[3,32,256]{2,1,0:T(8,128)S(1)}, s32[27,256]{1,0:T(8,128)}, f32[4,32,288]{1,0,2:T(4,128)S(1)}, /*index=5*/s32[]{:T(128)}, f32[]{:T(128)}, s32[]{:T(128)}) while((s32[]{:T(128)}, f32[9,32,256]{2,1,0:T(8,128)S(1)}, f32[3,32,256]{2,1,0:T(8,128)S(1)}, ...), condition=%wide.region_3.4_spmd.clone, body=%wide.region_0.3_spmd.clone.sunk | while | flops 21384960 | bytes 59322508 | solution.py:55
  76.2 2.9 multiply_dynamic-update-slice_fusion.15
  82.0 5.3 reduce_sum.22
  107.7 2.9 multiply_dynamic-update-slice_fusion.15
  113.5 5.3 reduce_sum.22
  139.3 2.9 multiply_dynamic-update-slice_fusion.15
  145.1 5.3 reduce_sum.22
  170.8 2.9 multiply_dynamic-update-slice_fusion.15
  176.6 5.3 reduce_sum.22
  202.4 2.9 multiply_dynamic-update-slice_fusion.15
  208.1 5.3 reduce_sum.22
  233.9 2.9 multiply_dynamic-update-slice_fusion.15
  239.7 5.3 reduce_sum.22
  265.5 2.9 multiply_dynamic-update-slice_fusion.15
  271.2 5.3 reduce_sum.22
  297.0 2.9 multiply_dynamic-update-slice_fusion.15
  302.8 5.3 reduce_sum.22
  328.6 2.9 multiply_dynamic-update-slice_fusion.15
  334.3 5.3 reduce_sum.22
  360.1 2.9 multiply_dynamic-update-slice_fusion.15
  365.9 5.3 reduce_sum.22
  391.7 2.9 multiply_dynamic-update-slice_fusion.15
  397.4 5.3 reduce_sum.22
  423.2 2.9 multiply_dynamic-update-slice_fusion.15
  429.0 5.3 reduce_sum.22
  454.7 2.9 multiply_dynamic-update-slice_fusion.15
  460.5 5.3 reduce_sum.22
  486.3 2.9 multiply_dynamic-update-slice_fusion.15
  492.1 5.3 reduce_sum.22
  517.8 2.9 multiply_dynamic-update-slice_fusion.15
  523.6 5.3 reduce_sum.22
  549.4 2.9 multiply_dynamic-update-slice_fusion.15
  555.1 5.3 reduce_sum.22
  580.9 2.9 multiply_dynamic-update-slice_fusion.15
  586.7 5.3 reduce_sum.22
  612.5 2.9 multiply_dynamic-update-slice_fusion.15
  618.2 5.3 reduce_sum.22
  644.0 2.9 multiply_dynamic-update-slice_fusion.15
  649.8 5.3 reduce_sum.22
  675.6 2.9 multiply_dynamic-update-slice_fusion.15
  681.3 5.3 reduce_sum.22
  707.1 2.9 multiply_dynamic-update-slice_fusion.15
  712.9 5.3 reduce_sum.22
  738.6 2.9 multiply_dynamic-update-slice_fusion.15
  744.4 5.3 reduce_sum.22
  770.2 2.9 multiply_dynamic-update-slice_fusion.15
  776.0 5.3 reduce_sum.22
  801.7 2.9 multiply_dynamic-update-slice_fusion.15
  807.5 5.3 reduce_sum.22
  833.3 2.9 multiply_dynamic-update-slice_fusion.15
  839.1 5.3 reduce_sum.22
  864.8 2.9 multiply_dynamic-update-slice_fusion.15
  870.6 5.3 reduce_sum.22
  902.1 5.3 reduce_sum.22
  911.2 308.2 %gather_fusion.2 = bf16[80896,121]{1,0:T(8,128)(2,1)} fusion(bf16[121,1280]{0,1:T(8,128)(2,1)S(1)} %pad_maximum_fusion, s32[80896]{0:T(1024)} %broadcast_clamp_fusion.1), kind=kCustom, calls=%fused_computation.2 | custom fusion | bytes 39477248 | tf_op jit(solution)/shard_map/jit(_take)/gather | solution.py:99
  1219.4 35.1 %fusion.7 = f32[256,121,1]{1,0,2:T(8,128)S(1)} fusion(bf16[316,256,121]{2,1,0:T(8,128)(2,1)} %bitcast.103, pred[316,256]{1,0:T(8,128)(4,1)S(1)} %copy-done.9, pred[316,256]{1,0:T(8,128)(4,1)S(1)} %copy-done.8, bf16[316,121,121]{2,0,1:T(8,128)(2,1)} %param.18), kind=kOutput, calls=%fused_computation.34 | convolution fusion | flops 2388373504 | bytes 29115640 | tf_op jit(solution)/shard_map/kol,okj->jl/dot_general | solution.py:101
  (648 shorter events, 652.0 us)
Async XLA Ops:
  0.0 1254.5 %copy-start = (f32[9,121,121]{2,1,0:T(8,128)S(1)}, f32[9,121,121]{2,1,0:T(8,128)}, u32[]{:S(2)}) copy-start(f32[9,121,121]{2,1,0:T(8,128)} %param.17) | copy-start | bytes 1581232
  0.0 41.1 %copy-start.7 = (s32[316,256]{1,0:T(8,128)S(1)}, s32[316,256]{1,0:T(8,128)}, u32[]{:S(2)}) copy-start(s32[316,256]{1,0:T(8,128)} %param.20) | copy-start | bytes 970756
  2.9 1.0 copy-start.6
  3.9 38.9 %copy-start.5 = (f32[3,32,256]{2,1,0:T(8,128)S(1)}, f32[3,32,256]{2,1,0:T(8,128)}, u32[]{:S(2)}) copy-start(f32[3,32,256]{2,1,0:T(8,128)} %param.14) | copy-start | bytes 294916
  5.5 37.3 %collective-permute-start.1 = (f32[4,32,16]{2,1,0:T(8,128)}, f32[4,32,16]{2,1,0:T(8,128)S(1)}, u32[]{:S(2)}, u32[]{:S(2)}) collective-permute-start(f32[4,32,16]{2,1,0:T(8,128)} %get-tuple-element.85), channel_id=1, source_target_pairs={{1,0},{2,1},{3,2},{4,3},{5,4},{6,5},{7,6},{8,7},{9,8},{10,9},{11,1... | collective-permute-start | bytes 24584 | tf_op jit(solution)/shard_map/ppermute | solution.py:20
  16.6 26.2 %collective-permute-start = (f32[4,32,16]{2,1,0:T(8,128)S(1)}, f32[4,32,16]{2,1,0:T(8,128)S(1)}, u32[]{:S(2)}, u32[]{:S(2)}) collective-permute-start(f32[4,32,16]{2,1,0:T(8,128)S(1)} %get-tuple-element.84), channel_id=1, source_target_pairs={{0,1},{1,2},{2,3},{3,4},{4,5},{5,6},{6,7},{7,8},{8,9},{9,10},{10,1... | collective-permute-start | bytes 24584 | tf_op jit(solution)/shard_map/ppermute | solution.py:19
  24.2 4.8 copy-start.2
  36.5 11.1 all-to-all-start
  48.4 861.6 %all-to-all-start.1 = ((bf16[8,32,4,121]{3,2,0,1:T(4,128)(2,1)}), bf16[8,32,4,121]{3,2,0,1:T(4,128)(2,1)}, u32[]{:S(2)}, u32[]{:S(2)}) async-start(bf16[8,32,4,121]{3,2,0,1:T(4,128)(2,1)} %copy.72), calls=%async_computation.1 | async-start | bytes 524288 | tf_op jit(solution)/shard_map/all_to_all | solution.py:90
  70.8 8.3 copy-start.1
  102.4 8.3 copy-start.1
  133.9 8.3 copy-start.1
  165.5 8.3 copy-start.1
  197.0 8.3 copy-start.1
  228.6 8.3 copy-start.1
  260.1 8.3 copy-start.1
  291.6 8.3 copy-start.1
  323.2 8.3 copy-start.1
  354.7 8.3 copy-start.1
  386.3 8.3 copy-start.1
  417.8 8.3 copy-start.1
  449.4 8.3 copy-start.1
  480.9 8.3 copy-start.1
  512.5 8.3 copy-start.1
  544.0 8.3 copy-start.1
  575.6 8.3 copy-start.1
  607.1 8.3 copy-start.1
  638.6 8.3 copy-start.1
  670.2 8.3 copy-start.1
  701.7 8.3 copy-start.1
  733.3 8.3 copy-start.1
  764.8 8.3 copy-start.1
  796.4 8.3 copy-start.1
  827.9 8.3 copy-start.1
  859.5 8.3 copy-start.1
  891.0 8.3 copy-start.1
  911.2 308.3 %copy-start.8 = (pred[316,256]{1,0:T(8,128)(4,1)S(1)}, pred[316,256]{1,0:T(8,128)(4,1)}, u32[]{:S(2)}) copy-start(pred[316,256]{1,0:T(8,128)(4,1)} %get-tuple-element.82) | copy-start | bytes 242692
  911.2 308.2 %copy-start.9 = (pred[316,256]{1,0:T(8,128)(4,1)S(1)}, pred[316,256]{1,0:T(8,128)(4,1)}, u32[]{:S(2)}) copy-start(pred[316,256]{1,0:T(8,128)(4,1)} %get-tuple-element.83) | copy-start | bytes 242692
  1219.4 36.2 %copy-start.3 = (bf16[121,32,256]{0,1,2:T(8,128)(2,1)S(1)}, bf16[121,32,256]{0,1,2:T(8,128)(2,1)}, u32[]{:S(2)}) copy-start(bf16[121,32,256]{0,1,2:T(8,128)(2,1)} %copy-done.2) | copy-start | bytes 5947396
  1219.4 36.2 %copy-start.4 = (f32[9,32,256]{1,0,2:T(8,128)S(1)}, f32[9,32,256]{1,0,2:T(8,128)}, u32[]{:S(2)}) copy-start(f32[9,32,256]{1,0,2:T(8,128)} %copy.79) | copy-start | bytes 884740
where the time goes:
time: 1270 us; the launch traced here: 1260 us
  other arithmetic  822 us (65%)
  local copies, waits for them, and re-layouts  360 us (28%)
  matrix products  44.5 us (4%)
  starting transfers between devices  25 us (2%)
    while x216, other arithmetic  492 us
    gather x1, local copies, waits for them, and re-layouts, shards(): jnp.take(source_pool, jnp.clip(m2l_list, 0, source_pool.shape[1] - 1), ax...  308 us
    reduce_sum x27, other arithmetic, one_slot(): return (running + jnp.sum(pair_terms, axis=2), None)  143 us
    sub x27, other arithmetic, one_slot(): offsets = own_src[:3, :, None, :] - picked[:3, None, :, :]  60.6 us
    another operation x27, other arithmetic, one_slot(): jnp.stack([charge * inverse, weighted * along_x, weighted * along_y, weig...  38.8 us
    dot_general x1, matrix products, shards(): jnp.einsum('kol,okj->jl', gathered, m2l_ops, preferred_element_type=jnp.f...  35.1 us
    select_n x27, other arithmetic, one_slot(): picked = jnp.where(usable[None, None, :], picked, 0.0)  33.8 us
    gather x27, local copies, waits for them, and re-layouts, one_slot(): jnp.take(extended, jnp.clip(slot_row, 0, extended.shape[2] - 1), axis=2)  26.8 us
  transfers between devices with their start and end apart: 4, of which 1 were waited for; matrix products, arithmetic and copies ran while one was open for 69% of the time, Pallas kernels for 0%

commit v1 on v0

v1 whole, which is shorter than its diff:
```python
import functools

import jax
import jax.numpy as jnp
from jax import lax
from jax.experimental import pallas as pl
from jax.experimental.pallas import tpu as pltpu
from jax.sharding import PartitionSpec as P

F32 = jnp.float32
BF = jnp.bfloat16
HALO = 16
NB, LAG, M = 6, 5, 80


def padded(value, axes, width):
    count, length = (lax.axis_size(axes), value.shape[2])
    up = [(i, (i + 1) % count) for i in range(count - 1)]
    down = [(j, i) for i, j in up]
    before = lax.ppermute(value[:, :, length - width :], axes, up)
    after = lax.ppermute(value[:, :, :width], axes, down)
    return jnp.concatenate([before, value, after], axis=2)


def near_kernel(near_ref, own_ref, ext_ref, out_ref, picked, keys_s, srt, nsm):
    n_near, leaves = near_ref.shape
    atoms = 32
    blocks = ext_ref.shape[1] // 128
    for lb in range(2):
        lanes = slice(lb * 128, lb * 128 + 128)
        pos = srt[:, lanes]
        safe = jnp.maximum(pos, 0)
        lane = safe & 127
        blk = safe >> 7
        for r in range(0, 32, 8):
            cnt = None
            for k in range(blocks):
                t = jnp.take_along_axis(ext_ref[128:136, k * 128:k * 128 + 128], lane[r:r + 8], axis=1, mode="promise_in_bounds")
                cnt = t if cnt is None else jnp.where(blk[r:r + 8] == k, t, cnt)
            key = jnp.where(pos[r:r + 8] >= 0, cnt.astype(jnp.int32) * 512 + safe[r:r + 8], 0)
            keys_s[lb, r:r + 8, :] = key
    ks = [keys_s[:, r, :] for r in range(32)]
    for a, b in batcher(32):
        hi = jnp.maximum(ks[a], ks[b]); lo = jnp.minimum(ks[a], ks[b])
        ks[a], ks[b] = hi, lo
    for r in range(32):
        keys_s[:, r, :] = ks[r]
    for r in range(n_near):
        for lb in range(2):
            m = jnp.max(ks[r][lb:lb + 1].astype(F32))
            nsm[lb, r] = m.astype(jnp.int32) >> 9

    for lb in range(2):
        lanes = slice(lb * 128, lb * 128 + 128)
        def gather(n, _):
            key = keys_s[lb, pl.ds(n, 1), :]
            pos = jnp.broadcast_to(key & 511, (8, 128))
            lane = pos & 127
            blk = pos >> 7
            live = jnp.broadcast_to(key, (8, 128)) > 0
            for c in range(4):
                for r in range(0, atoms, 8):
                    v = None
                    for k in range(blocks):
                        t = jnp.take_along_axis(ext_ref[c * 32 + r:c * 32 + r + 8, k * 128:k * 128 + 128], lane, axis=1, mode="promise_in_bounds")
                        v = t if v is None else jnp.where(blk == k, t, v)
                    if c == 3:
                        v = jnp.where(live, v, 0.0)
                    picked[n, c * 32 + r:c * 32 + r + 8, :] = v
            return 0
        lax.fori_loop(0, n_near, gather, 0)
        AG = 2
        for a0 in range(0, atoms, 8 * AG):
            own = [[own_ref[c * 32 + a0 + 8 * g:c * 32 + a0 + 8 * g + 8, lanes] for c in range(3)] for g in range(AG)]
            def entry(n, carry):
                def chunk(k, carry):
                    carry = list(carry)
                    for bb in range(4):
                        b = k * 4 + bb
                        src = [picked[n, pl.ds(c * 32 + b, 1), :] for c in range(4)]
                        for g in range(AG):
                            dx = own[g][0] - src[0]
                            dy = own[g][1] - src[1]
                            dz = own[g][2] - src[2]
                            w = lax.rsqrt(dx * dx + dy * dy + (dz * dz + 0.25))
                            w2 = w * w
                            qw = src[3] * w
                            q3 = qw * w2
                            s = q3 * w2
                            sx = s * dx
                            sy = s * dy
                            acc = carry[g * 10:g * 10 + 10]
                            new = [qw, q3 * dx, q3 * dy, q3 * dz, q3, sx * dx, sy * dy, sx * dy, sx * dz, sy * dz]
                            carry[g * 10:g * 10 + 10] = [p + t for p, t in zip(acc, new)]
                    return tuple(carry)
                return lax.fori_loop(0, (nsm[lb, n] + 3) // 4, chunk, carry)
            zero = jnp.zeros((8, 128), F32)
            res = lax.fori_loop(0, n_near, entry, tuple([zero] * (10 * AG)))
            for g in range(AG):
                p, gx, gy, gz, q3, xx, yy, xy, xz, yz = res[g * 10:g * 10 + 10]
                final = [p, gx, gy, gz, q3 - 3.0 * xx, q3 - 3.0 * yy, -3.0 * xy, -3.0 * xz, -3.0 * yz]
                for c in range(9):
                    out_ref[c, a0 + 8 * g:a0 + 8 * g + 8, lanes] = final[c]

def batcher(n):
    out = []
    p = 1
    while p < n:
        k = p
        while k >= 1:
            for j in range(k % p, n - k, 2 * k):
                for i in range(min(k, n - j - k)):
                    if (i + j) // (2 * p) == (i + j + k) // (2 * p):
                        out.append((i + j, i + j + k))
            k //= 2
        p *= 2
    return out

def near(near_rows, own, ext):
    V=pltpu.VMEM
    srt = jnp.pad(near_rows, ((0, 32 - near_rows.shape[0]), (0, 0)), constant_values=-1)
    e = jnp.pad(ext, ((0,0),(0,0),(0, 384 - ext.shape[2]))).reshape(160, 384)
    def kern(near_ref, srt, own_ref, ext_ref, out_ref, picked, keys_s, nsm):
        near_kernel(near_ref, own_ref, ext_ref, out_ref, picked, keys_s, srt, nsm)
    return pl.pallas_call(kern, out_shape=jax.ShapeDtypeStruct((9, 32, 256), F32),
        in_specs=[pl.BlockSpec(memory_space=V)]*4, out_specs=pl.BlockSpec(memory_space=V),
        scratch_shapes=[V((27, 128, 128), F32), V((2, 32, 128), jnp.int32), pltpu.SMEM((2, 32), jnp.int32)],
        compiler_params=pltpu.CompilerParams(vmem_limit_bytes=24*1024*1024))(near_rows, srt, own.reshape(96, 256), e)

def m2l_inner(idx_ref, ops_ref, own_ref, inc_ref, out_ref, idx_s, pool, ptmp, xs, t_s, g_s, acc, *ra):
    n_off, leaves = idx_ref.shape
    coef = ops_ref.shape[0]
    n_pad = idx_s.shape[0]
    full = n_off // 16
    ra = [ra[:NB], ra[NB:]]
    idx_s[...] = jnp.full_like(idx_s, -1)
    idx_s[0:n_off, :] = idx_ref[...]
    ptmp[...] = jnp.zeros_like(ptmp)
    for h in range(5):
        if h == 0:
            ptmp[0:coef, :] = own_ref[...].astype(F32)
        else:
            ptmp[0:coef, :] = inc_ref[(h - 1) * 256:h * 256, :].astype(F32).T
        for c in range(8):
            pool[c, h * 16:(h + 1) * 16, :] = ptmp[c * 16:(c + 1) * 16, :].astype(BF)
    t_s[...] = jnp.zeros_like(t_s)
    g_s[...] = jnp.zeros_like(g_s)
    acc[...] = jnp.zeros_like(acc)
    xs[...] = jnp.zeros_like(xs)
    xs[0:coef * 16, 0:coef] = ops_ref[:, 0:16, :].astype(F32).reshape(coef * 16, coef)
    tail = n_off - full * 16
    for k in range(coef):
        xs[4096 + k * 16:4096 + k * 16 + tail, 0:coef] = ops_ref[k, full * 16:n_off, :].astype(F32)
    iota = lax.broadcasted_iota(jnp.int32, (256, 256), 0).astype(F32).astype(BF)
    one = jnp.ones((256, 256), BF)
    zero = jnp.zeros((256, 256), BF)
    half = coef - 64

    def hot(o):
        row = idx_s[pl.ds(o, 1), :]
        lo = jnp.where(row >= 0, row & 255, -1).astype(F32).astype(BF)
        return jnp.where(iota == lo, one, zero)

    def relayout(b):
        c = jnp.minimum(b // 2 + 1, full - 1)
        k0 = lax.rem(b, 2) * half
        xs[pl.ds(pl.multiple_of(lax.rem(b // 2 + 1, 2) * 2048 + k0 * 16, 16), 1024), 0:coef] = ops_ref[pl.ds(k0, 64), pl.ds(pl.multiple_of(c * 16, 16), 16), :].astype(F32).reshape(1024, coef)

    def take_ops(b, w):
        c = b // 2
        slot = jnp.where(c == full, 2, lax.rem(c, 2))
        o8 = lax.rem(b, 2) * 8
        for m in range(2):
            for u in range(2):
                x = xs[pl.ds(slot * 2048 + o8 + 4 * w + 2 * m + u, 128, stride=16), :]
                t_s[w, m, 0:128, 128 * u:128 * u + 128] = x.astype(BF).T

    def pop_dot1(m, slot, u, c, o, buf):
        r = pltpu.matmul_pop(buf)
        hi = idx_s[pl.ds(o, 1), :] >> 8
        g = r[0:16]
        for h in range(1, 5):
            g = jnp.where(hi == h, r[16 * h:16 * h + 16], g)
        g_s[slot, m, u * 128 + c * 16:u * 128 + (c + 1) * 16, :] = g.astype(BF)

    def pop_dot2(m, part, buf):
        acc[m, part * M:(part + 1) * M, :] += pltpu.matmul_pop(buf)

    seq = [("a", 0, c) for c in range(8)] + [("d", 0, 0), ("d", 0, 1)] + [("a", 1, c) for c in range(8)]

    def pop(m, w, item, base, buf):
        kind, u, c = item
        if kind == "a":
            pop_dot1(m, w, u, c, base + 2 * m + u, buf)
        else:
            pop_dot2(m, c, buf)

    def issue(b, w, s, base, last=False):
        kind, u, c = seq[s]
        for m in range(2):
            buf = ra[m][s % NB]
            if kind == "a":
                pltpu.matmul_acc_lhs(buf, pool[c], load_staged_rhs=0 if c == 0 else None)
            else:
                pltpu.matmul_acc_lhs(buf, t_s[1 - w, m, c * M:(c + 1) * M, :], load_staged_rhs=1 if c == 0 else None)

    n_body = n_pad // 8
    for m in range(2):
        pltpu.matmul_push_rhs(hot(2 * m), 0, m)
    for m in range(2):
        pltpu.matmul_push_rhs(zero, 1, m)
        for s in range(len(seq) - LAG, len(seq)):
            pltpu.matmul_acc_lhs(ra[m][s % NB], pool[0], load_staged_rhs=1 if s == len(seq) - LAG else None)

    def body(b, _):
        for w in range(2):
            base = b * 8 + 4 * w
            prev = jnp.maximum(base - 4, 0)
            for s in range(len(seq)):
                issue(b, w, s, base)
                if s == 0:
                    for m in range(2):
                        pltpu.matmul_push_rhs(hot(base + 2 * m + 1), 0, m)
                if s == LAG:
                    for m in range(2):
                        pltpu.matmul_push_rhs(g_s[1 - w, m], 1, m)
                if s == 10:
                    for m in range(2):
                        pltpu.matmul_push_rhs(hot(jnp.minimum(base + 4 + 2 * m, n_pad - 1)), 0, m)
                p = s - LAG
                for m in range(2):
                    if p >= 0:
                        pop(m, w, seq[p], base, ra[m][p % NB])
                    else:
                        pop(m, 1 - w, seq[p + len(seq)], prev, ra[m][(p + len(seq)) % NB])
                if s == 11:
                    take_ops(b, w)
        relayout(b)
        return 0

    lax.fori_loop(0, n_body, body, 0)
    nb = len(seq)
    for s in range(nb - LAG, nb):
        for m in range(2):
            pop(m, 1, seq[s], n_pad - 4, ra[m][s % NB])
    for m in range(2):
        pltpu.matmul_acc_lhs(ra[m][0], pool[0], load_staged_rhs=0)
    junk = [pltpu.matmul_pop(ra[m][0]) for m in range(2)]
    for m in range(2):
        pltpu.matmul_push_rhs(g_s[1, m], 1, m)
        for c in range(2):
            pltpu.matmul_acc_lhs(ra[m][c], t_s[1, m, c * M:(c + 1) * M, :], load_staged_rhs=1 if c == 0 else None)
    for m in range(2):
        for c in range(2):
            pop_dot2(m, c, ra[m][c])
    out_ref[...] = acc[0, 0:coef, :] + acc[1, 0:coef, :]

def m2l_kernel(*refs):
    accs = [pltpu.ACC(m)((M, 256), F32) for m in range(2) for _ in range(NB)]
    pl.run_scoped(functools.partial(m2l_inner, *refs), *accs)

def m2l(idx, ops, own, inc):
    n_off = idx.shape[0]
    coef = ops.shape[0]
    n_pad = -(-n_off // 8) * 8
    V = pltpu.VMEM
    return pl.pallas_call(
        m2l_kernel,
        out_shape=jax.ShapeDtypeStruct((coef, 256), F32),
        in_specs=[pl.BlockSpec(memory_space=V)] * 4,
        out_specs=pl.BlockSpec(memory_space=V),
        scratch_shapes=[V((n_pad, 256), jnp.int32), V((8, M, 256), BF), V((128, 256), F32), V((3 * 2048, 128), F32),
                        V((2, 2, 2 * M, 256), BF), V((2, 2, 256, 256), BF), V((2, 2 * M, 256), F32)],
        compiler_params=pltpu.CompilerParams(vmem_limit_bytes=40*1024*1024),
    )(idx, ops, own, inc)


def shards(
    multipoles,
    harmonics,
    positions,
    atom_counts,
    source_ops,
    field_ops,
    m2l_ops,
    send_list,
    m2l_list,
    near_list,
):
    axes = ("grp", "dev")
    atoms, leaves = positions.shape[1:]
    slot_ids = lax.broadcasted_iota(jnp.int32, (atoms, leaves), 0)
    present = slot_ids < atom_counts[None, :]
    masked = jnp.where(present[None], multipoles, jnp.zeros_like(multipoles))
    counts = jnp.broadcast_to(atom_counts.astype(F32)[None, None, :], (1, atoms, leaves))
    own_src = jnp.concatenate([positions, masked[0:1].astype(F32), counts], axis=0)
    extended = padded(own_src, axes, HALO)
    sources = jnp.einsum("cal,kal->ckl", masked, harmonics, preferred_element_type=F32)
    moments = jnp.einsum("ckj,ckl->jl", source_ops, sources, precision=lax.Precision.HIGHEST).astype(BF)
    coef_count = moments.shape[0]
    send_rows = send_list[0]
    slot_count = send_rows.shape[1]
    peer_count = lax.axis_size(axes)
    flat_rows = send_rows.reshape(-1)
    outgoing = jnp.take(moments, jnp.clip(flat_rows, 0, None), axis=1)
    outgoing = jnp.where(flat_rows[None, :] >= 0, outgoing, jnp.zeros_like(outgoing))
    outgoing = outgoing.T.reshape(peer_count, slot_count, coef_count)
    groups = lax.axis_size("grp")
    sectioned = outgoing.reshape(groups, peer_count // groups, slot_count, coef_count)
    arrived = lax.all_to_all(
        lax.all_to_all(sectioned, "grp", split_axis=0, concat_axis=0, tiled=True),
        "dev",
        split_axis=1,
        concat_axis=1,
        tiled=True,
    )
    incoming = arrived.reshape(peer_count * slot_count, coef_count)
    near_part = near(near_list, positions, extended)
    local_exp = m2l(m2l_list, m2l_ops.transpose(1, 0, 2), moments, incoming)
    derived = jnp.einsum("ckj,jl->ckl", field_ops, local_exp, precision=lax.Precision.HIGHEST).astype(BF)
    far_part = jnp.einsum("ckl,kal->cal", derived, harmonics, preferred_element_type=F32)
    return jnp.where(present[None], far_part + near_part, 0.0)


def solution(mesh):
    placed = (
        P(None, None, ("grp", "dev")),
        P(None, None, ("grp", "dev")),
        P(None, None, ("grp", "dev")),
        P(("grp", "dev")),
        P(),
        P(),
        P(),
        P(("grp", "dev"), None, None),
        P(None, ("grp", "dev")),
        P(None, ("grp", "dev")),
    )
    inner = jax.shard_map(
        shards, mesh=mesh, in_specs=placed, out_specs=P(None, None, ("grp", "dev")), check_vma=False
    )

    def whole(*args):
        with jax.sharding.use_abstract_mesh(mesh.abstract_mesh):
            return inner(*args)

    return whole
```

time: 1270 us -> 148 us (0.12)
  other arithmetic: 822 us -> 4.33 us
  local copies, waits for them, and re-layouts: 360 us -> 18.3 us
  Pallas kernels: 0 us -> 80.9 us
  matrix products: 44.5 us -> 7.34 us
    while x216 -> x0, other arithmetic: 492 us -> none
    gather x28 -> x0, local copies, waits for them, and re-layouts: 335 us -> none  [the longest x1 308 us: shards(): jnp.take(source_pool, jnp.clip(m2l_list, 0, source_pool.shape[1] - 1), ax...]
    reduce_sum x27 -> x0, other arithmetic: 143 us -> none  [one_slot(): return (running + jnp.sum(pair_terms, axis=2), None)]
    pallas_call x0 -> x2, Pallas kernels: none -> 80.9 us  [the longest x1 41 us: m2l(): pl.pallas_call(m2l_kernel, out_shape=jax.ShapeDtypeStruct((coef, 256), F3...]
    sub x27 -> x0, other arithmetic: 60.6 us -> none  [one_slot(): offsets = own_src[:3, :, None, :] - picked[:3, None, :, :]]
    select_n x55 -> x1, other arithmetic: 53.1 us -> 0.76 us  [shards(): return jnp.where(present[None], far_part + near_part, 0.0)]
    another operation x27 -> x0, other arithmetic: 38.8 us -> none  [one_slot(): jnp.stack([charge * inverse, weighted * along_x, weighted * along_y, weig...]
    dot_general x3 -> x2, matrix products: 40.3 us -> 4.49 us  [the longest x1 2.53 us: shards(): jnp.einsum('ckl,kal->cal', derived, harmonics, preferred_element_type=F32)]
  transfers between devices with their start and end apart: 4 -> 3, of which waited for: 1 -> 1; matrix products, arithmetic and copies ran while one was open for 69% -> 0% of each run, Pallas kernels for 0% -> 27%
where the time goes in v1:
time: 148 us; the launch traced here: 147 us
  Pallas kernels  80.9 us (55%)
  starting transfers between devices  21 us (14%)
  local copies, waits for them, and re-layouts  18.3 us (12%)
  blocking collectives  12.4 us (8%)
  matrix products  7.34 us (5%)
  other arithmetic  4.33 us (3%)
  waiting for transfers between devices  2.67 us (2%)
    pallas_call x1, Pallas kernels, m2l(): pl.pallas_call(m2l_kernel, out_shape=jax.ShapeDtypeStruct((coef, 256), F3...  41 us
    pallas_call x1, Pallas kernels, near(): pl.pallas_call(kern, out_shape=jax.ShapeDtypeStruct((9, 32, 256), F32), i...  39.8 us
    all_to_all x1, blocking collectives, shards(): lax.all_to_all(sectioned, 'grp', split_axis=0, concat_axis=0, tiled=True)  12.4 us
    all_to_all x1, starting transfers between devices, shards(): lax.all_to_all(lax.all_to_all(sectioned, 'grp', split_axis=0, concat_axis...  11.2 us
    unnamed x15, local copies, waits for them, and re-layouts  8.15 us
    ppermute x1, starting transfers between devices, padded(): after = lax.ppermute(value[:, :, :width], axes, down)  6.82 us
    gather x1, local copies, waits for them, and re-layouts, shards(): outgoing = jnp.take(moments, jnp.clip(flat_rows, 0, None), axis=1)  3.21 us
    ppermute x1, starting transfers between devices, padded(): before = lax.ppermute(value[:, :, length - width:], axes, up)  3.06 us
  transfers between devices with their start and end apart: 3, of which 1 were waited for; matrix products, arithmetic and copies ran while one was open for 0% of the time, Pallas kernels for 27%

profile of v1, /device:TPU:1, one launch (start us, length us, event | category | flops | bytes accessed | tf_op | source)
XLA Modules:
  0.0 147.2 jit_solution(16230703370769375848)
XLA Ops:
  0.0 0.0 copy-start
  0.0 0.8 broadcast_maximum_fusion
  0.8 0.7 broadcast_compare_fusion
  1.4 0.7 iota_compare_fusion.1
  2.1 0.9 broadcast_select_fusion
  3.1 1.9 %copy.36 = bf16[9,32,256]{1,0,2:T(8,128)(2,1)} copy(bf16[9,32,256]{2,1,0:T(8,128)(2,1)S(1)} %broadcast_select_fusion) | data formatting | bytes 294912 | tf_op jit(solution)/shard_map/jit(_where)/select_n | solution.py:294
  4.9 4.3 %copy.37 = bf16[121,32,256]{0,1,2:T(8,128)(2,1)S(1)} copy(bf16[121,32,256]{2,1,0:T(8,128)(2,1)} %param.11) | data formatting | bytes 3964928 | tf_op args[1]
  9.2 0.0 copy-start.5
  9.2 2.0 %convolution_bitcast_fusion = f32[9,121,256]{1,0,2:T(8,128)S(1)} fusion(bf16[9,32,256]{1,0,2:T(8,128)(2,1)} %copy.36, bf16[121,32,256]{0,1,2:T(8,128)(2,1)S(1)} %copy.37), kind=kOutput, calls=%fused_computation.1 | convolution fusion | flops 17842176 | bytes 3245056 | tf_op jit(solution)/shard_map/cal,kal->ckl/dot_general | solution.py:298
  11.2 0.0 copy-done.5
  11.2 1.6 %fusion.9.refs_2_ = bf16[121,256]{1,0:T(8,128)(2,1)S(1)} fusion(f32[9,121,121]{2,1,0:T(8,128)S(1)} %copy-done.5, f32[9,121,256]{1,0,2:T(8,128)S(1)} %convolution_bitcast_fusion), kind=kOutput, calls=%fused_computation.8 | convolution fusion | flops 404825344 | bytes 1704164 | tf_op jit(solution)/shard_map/ckj,ckl->jl/dot_general | solution.py:299
  12.8 0.1 copy.43
  12.9 0.1 copy.42
  13.1 0.1 reshape.67
  13.2 0.2 copy.40
  13.4 0.1 ge.23
  13.5 0.2 copy.41
  13.7 0.1 le.16
  13.8 0.0 copy-start.6
  13.9 0.0 copy-start.2
  13.9 0.0 copy-start.4
  13.9 3.2 %gather_fusion = bf16[1024,121]{1,0:T(8,128)(2,1)S(1)} fusion(bf16[121,256]{0,1:T(8,128)(2,1)S(1)} %copy.43, s32[1024]{0:T(1024)S(1)} %broadcast_clamp_fusion), kind=kCustom, calls=%fused_computation | custom fusion | bytes 499712 | tf_op jit(solution)/shard_map/jit(_take)/gather | solution.py:305
  17.1 0.3 select_select_fusion
  17.4 0.0 copy-start.3
  17.5 12.4 %all_to_all.10 = bf16[8,32,4,121]{3,2,1,0:T(4,128)(2,1)S(1)} all-to-all(bf16[8,32,4,121]{3,2,1,0:T(4,128)(2,1)S(1)} %bitcast.33), channel_id=1, replica_groups=mesh['grp'=8,'dev'=32] {'grp'}, dimensions={0} | all-to-all | bytes 495616 | tf_op jit(solution)/shard_map/all_to_all | solution.py:311
  29.9 0.8 copy.44
  30.7 11.2 %all-to-all-start.1 = ((bf16[8,32,4,121]{3,2,0,1:T(4,128)(2,1)}), bf16[8,32,4,121]{3,2,0,1:T(4,128)(2,1)}, u32[]{:S(2)}, u32[]{:S(2)}) async-start(bf16[8,32,4,121]{3,2,0,1:T(4,128)(2,1)} %copy.44), calls=%async_computation.1 | async-start | bytes 524288 | tf_op jit(solution)/shard_map/all_to_all | solution.py:310
  41.8 0.0 copy-done.6
  41.9 0.0 copy-done.2
  41.9 0.1 fusion.21
  42.0 3.1 %collective-permute-start = (f32[5,32,16]{2,1,0:T(8,128)S(1)}, f32[5,32,16]{2,1,0:T(8,128)S(1)}, u32[]{:S(2)}, u32[]{:S(2)}) collective-permute-start(f32[5,32,16]{2,1,0:T(8,128)S(1)} %get-tuple-element.5), channel_id=1, source_target_pairs={{0,1},{1,2},{2,3},{3,4},{4,5},{5,6},{6,7},{7,8},{8,9},{9,10},{10,1... | collective-permute-start | bytes 30728 | tf_op jit(solution)/shard_map/ppermute | solution.py:20
  45.1 6.8 %collective-permute-start.1 = (f32[5,32,16]{2,1,0:T(8,128)S(1)}, f32[5,32,16]{2,1,0:T(8,128)S(1)}, u32[]{:S(2)}, u32[]{:S(2)}) collective-permute-start(f32[5,32,16]{2,1,0:T(8,128)S(1)} %get-tuple-element.6), channel_id=1, source_target_pairs={{1,0},{2,1},{3,2},{4,3},{5,4},{6,5},{7,6},{8,7},{9,8},{10,9},{11,1... | collective-permute-start | bytes 30728 | tf_op jit(solution)/shard_map/ppermute | solution.py:21
  51.9 0.0 copy-done.4
  51.9 2.7 %collective-permute-done = f32[5,32,16]{2,1,0:T(8,128)S(1)} collective-permute-done((f32[5,32,16]{2,1,0:T(8,128)S(1)}, f32[5,32,16]{2,1,0:T(8,128)S(1)}, u32[]{:S(2)}, u32[]{:S(2)}) %collective-permute-start) | collective-permute-done | bytes 10272 | tf_op jit(solution)/shard_map/ppermute | solution.py:20
  54.6 0.0 collective-permute-done.1
  54.6 0.2 select_maximum_fusion
  54.7 39.8 %shard_map.101 = f32[9,32,256]{2,1,0:T(8,128)S(1)} custom-call(s32[27,256]{1,0:T(8,128)S(1)} %copy-done.4, s32[32,256]{1,0:T(8,128)S(1)} %pad.8.srt, f32[96,256]{1,0:T(8,128)S(1)} %bitcast.32, f32[160,384]{1,0:T(8,128)S(1)} %bitcast.31), custom_call_target="tpu_custom_call" | custom-call | tf_op jit(solution)/shard_map/pallas_call | solution.py:125
  94.6 0.0 all-to-all-done.1
  94.6 1.0 copy.45
  95.6 0.0 copy-done.3
  95.7 0.0 copy-start.1
  95.7 3.8 %copy-done.1 = bf16[316,121,121]{2,0,1:T(8,128)(2,1)S(1)} copy-done((bf16[316,121,121]{2,0,1:T(8,128)(2,1)S(1)}, bf16[316,121,121]{2,0,1:T(8,128)(2,1)}, u32[]{:S(2)}) %copy-start.1) | copy-done | bytes 9253136
  99.5 41.0 %shard_map.100 = f32[121,256]{1,0:T(8,128)S(1)} custom-call(s32[316,256]{1,0:T(8,128)S(1)} %copy-done.3, bf16[121,316,121]{2,1,0:T(8,128)(2,1)S(1)} %bitcast.29, bf16[121,256]{1,0:T(8,128)(2,1)S(1)} %fusion.9.refs_2_, bf16[1024,121]{1,0:T(8,128)(2,1)S(1)} %bitcast.30), custom_call_target="tpu_custom_call" | custom-call | tf_op jit(solution)/shard_map/pallas_call | solution.py:267
  140.5 0.0 copy-done
  140.5 1.3 fusion
  141.8 2.5 %fusion.12 = f32[256,9,32]{2,1,0:T(8,128)} fusion(bf16[121,32,256]{0,1,2:T(8,128)(2,1)S(1)} %copy.37, bf16[9,121,256]{1,2,0:T(8,128)(2,1)S(1)} %fusion), kind=kOutput, calls=%fused_computation.9 | convolution fusion | flops 17842176 | bytes 2834944 | tf_op jit(solution)/shard_map/ckl,kal->cal/dot_general | solution.py:321
  144.3 2.1 %copy.49 = f32[256,9,32]{0,2,1:T(8,128)S(1)} copy(f32[256,9,32]{2,1,0:T(8,128)} %fusion.12) | data formatting | bytes 589824 | tf_op jit(solution)/shard_map/ckl,kal->cal/dot_general | solution.py:321
  146.4 0.8 fusion.14
  (6 shorter events, 0.0 us)
Async XLA Ops:
  0.0 140.5 %copy-start = (f32[9,121,121]{2,1,0:T(8,128)S(1)}, f32[9,121,121]{2,1,0:T(8,128)}, u32[]{:S(2)}) copy-start(f32[9,121,121]{2,1,0:T(8,128)} %param.15) | copy-start | bytes 1581232
  9.2 2.0 %copy-start.5 = (f32[9,121,121]{2,1,0:T(8,128)S(1)}, f32[9,121,121]{2,1,0:T(8,128)}, u32[]{:S(2)}) copy-start(f32[9,121,121]{2,1,0:T(8,128)} %param.14) | copy-start | bytes 1581232
  13.8 28.0 %copy-start.6 = (s32[256]{0:T(256)S(1)}, s32[256]{0:T(256)}, u32[]{:S(2)}) copy-start(s32[256]{0:T(256)} %param.13) | copy-start | bytes 3076
  13.9 28.0 %copy-start.2 = (f32[3,32,256]{2,1,0:T(8,128)S(1)}, f32[3,32,256]{2,1,0:T(8,128)}, u32[]{:S(2)}) copy-start(f32[3,32,256]{2,1,0:T(8,128)} %param.12) | copy-start | bytes 294916
  13.9 38.0 %copy-start.4 = (s32[27,256]{1,0:T(8,128)S(1)}, s32[27,256]{1,0:T(8,128)}, u32[]{:S(2)}) copy-start(s32[27,256]{1,0:T(8,128)} %near_ref.1) | copy-start | bytes 82948
  17.4 78.2 %copy-start.3 = (s32[316,256]{1,0:T(8,128)S(1)}, s32[316,256]{1,0:T(8,128)}, u32[]{:S(2)}) copy-start(s32[316,256]{1,0:T(8,128)} %refs_0_.1) | copy-start | bytes 970756
  30.7 63.9 %all-to-all-start.1 = ((bf16[8,32,4,121]{3,2,0,1:T(4,128)(2,1)}), bf16[8,32,4,121]{3,2,0,1:T(4,128)(2,1)}, u32[]{:S(2)}, u32[]{:S(2)}) async-start(bf16[8,32,4,121]{3,2,0,1:T(4,128)(2,1)} %copy.44), calls=%async_computation.1 | async-start | bytes 524288 | tf_op jit(solution)/shard_map/all_to_all | solution.py:310
  42.0 12.6 %collective-permute-start = (f32[5,32,16]{2,1,0:T(8,128)S(1)}, f32[5,32,16]{2,1,0:T(8,128)S(1)}, u32[]{:S(2)}, u32[]{:S(2)}) collective-permute-start(f32[5,32,16]{2,1,0:T(8,128)S(1)} %get-tuple-element.5), channel_id=1, source_target_pairs={{0,1},{1,2},{2,3},{3,4},{4,5},{5,6},{6,7},{7,8},{8,9},{9,10},{10,1... | collective-permute-start | bytes 30728 | tf_op jit(solution)/shard_map/ppermute | solution.py:20
  45.1 9.5 %collective-permute-start.1 = (f32[5,32,16]{2,1,0:T(8,128)S(1)}, f32[5,32,16]{2,1,0:T(8,128)S(1)}, u32[]{:S(2)}, u32[]{:S(2)}) collective-permute-start(f32[5,32,16]{2,1,0:T(8,128)S(1)} %get-tuple-element.6), channel_id=1, source_target_pairs={{1,0},{2,1},{3,2},{4,3},{5,4},{6,5},{7,6},{8,7},{9,8},{10,9},{11,1... | collective-permute-start | bytes 30728 | tf_op jit(solution)/shard_map/ppermute | solution.py:21
  95.7 3.8 %copy-start.1 = (bf16[316,121,121]{2,0,1:T(8,128)(2,1)S(1)}, bf16[316,121,121]{2,0,1:T(8,128)(2,1)}, u32[]{:S(2)}) copy-start(bf16[316,121,121]{2,0,1:T(8,128)(2,1)} %param.16) | copy-start | bytes 27759340

commit v2 on v1

v2 whole, which is shorter than its diff:
```python
import functools

import jax
import jax.numpy as jnp
from jax import lax
from jax.experimental import pallas as pl
from jax.experimental.pallas import tpu as pltpu
from jax.sharding import PartitionSpec as P

F32 = jnp.float32
BF = jnp.bfloat16
HALO = 16
def padded(value, axes, width):
    count, length = (lax.axis_size(axes), value.shape[2])
    up = [(i, (i + 1) % count) for i in range(count - 1)]
    down = [(j, i) for i, j in up]
    before = lax.ppermute(value[:, :, length - width :], axes, up)
    after = lax.ppermute(value[:, :, :width], axes, down)
    return jnp.concatenate([before, value, after], axis=2)


NB, LAG, M = 6, 5, 80
STEP = 4


def batcher(n):
    out = []
    p = 1
    while p < n:
        k = p
        while k >= 1:
            for j in range(k % p, n - k, 2 * k):
                for i in range(min(k, n - j - k)):
                    if (i + j) // (2 * p) == (i + j + k) // (2 * p):
                        out.append((i + j, i + j + k))
            k //= 2
        p *= 2
    return out


def take_lanes(ref, row, lane, blk, blocks):
    value = None
    for k in range(blocks):
        t = jnp.take_along_axis(
            ref[row : row + 8, k * 128 : k * 128 + 128], lane, axis=1, mode="promise_in_bounds"
        )
        value = t if value is None else jnp.where(blk == k, t, value)
    return value


def near_setup(near_ref, own_ref, ext_ref, keys_s, picked, own_s, nacc, cnt_s):
    blocks = ext_ref.shape[1] // 128
    n_near = picked.shape[1] - 1
    nacc[...] = jnp.zeros_like(nacc)
    for lb in range(2):
        lanes = slice(lb * 128, lb * 128 + 128)
        own_s[lb] = own_ref[:, lanes]
        picked[lb, n_near] = jnp.zeros((128, 128), F32)
        for r in range(0, 32, 8):
            pos = near_ref[r : r + 8, lanes]
            safe = jnp.maximum(pos, 0)
            count = take_lanes(ext_ref, 128, safe & 127, safe >> 7, blocks)
            keys_s[lb, r : r + 8, :] = jnp.where(pos >= 0, count.astype(jnp.int32) * 512 + safe, 0)
    ks = [keys_s[:, r, :] for r in range(32)]
    for a, b in batcher(32):
        ks[a], ks[b] = jnp.maximum(ks[a], ks[b]), jnp.minimum(ks[a], ks[b])
    total = jnp.int32(0)
    for r in range(32):
        keys_s[:, r, :] = ks[r]
    for r in range(n_near):
        for lb in range(2):
            top = jnp.max(ks[r][lb : lb + 1].astype(F32)).astype(jnp.int32) >> 9
            chunks = (top + STEP - 1) // STEP
            cnt_s[lb, r] = chunks
            total += chunks
    for lb in range(2):
        cnt_s[lb, n_near] = 0

    def gather(n, _):
        for lb in range(2):
            key = jnp.broadcast_to(keys_s[lb, pl.ds(n, 1), :], (8, 128))
            pos = key & 511
            for c in range(4):
                for r in range(0, 32, 8):
                    v = take_lanes(ext_ref, c * 32 + r, pos & 127, pos >> 7, blocks)
                    if c == 3:
                        v = jnp.where(key > 0, v, 0.0)
                    picked[lb, n, c * 32 + r : c * 32 + r + 8, :] = v
        return 0

    lax.fori_loop(0, n_near, gather, 0)
    return total


def near_item(state, picked, own_s, nacc, cnt_s):
    lb, n, k = state
    n_near = picked.shape[1] - 1
    for g in range(4):
        own = [own_s[lb, c * 32 + 8 * g : c * 32 + 8 * g + 8, :] for c in range(3)]
        acc = [nacc[lb, g, i] for i in range(10)]
        for bb in range(STEP):
            src = [picked[lb, n, pl.ds(c * 32 + k * STEP + bb, 1), :] for c in range(4)]
            dx = own[0] - src[0]
            dy = own[1] - src[1]
            dz = own[2] - src[2]
            w = lax.rsqrt(dx * dx + dy * dy + (dz * dz + 0.25))
            w2 = w * w
            qw = src[3] * w
            q3 = qw * w2
            s = q3 * w2
            sx = s * dx
            sy = s * dy
            new = [qw, q3 * dx, q3 * dy, q3 * dz, q3, sx * dx, sy * dy, sx * dy, sx * dz, sy * dz]
            acc = [p + t for p, t in zip(acc, new)]
        for i in range(10):
            nacc[lb, g, i] = acc[i]
    k1 = k + 1
    over = k1 >= cnt_s[lb, n]
    n1 = jnp.where(over, n + 1, n)
    k1 = jnp.where(over, 0, k1)
    out = cnt_s[lb, jnp.minimum(n1, n_near)] == 0
    done = out & (lb == 1)
    lb1 = jnp.where(out, 1, lb)
    n1 = jnp.where(out, jnp.where(done, n_near, 0), n1)
    n1 = jnp.where(cnt_s[lb1, n1] == 0, n_near, n1)
    return lb1, n1, k1


def near_first(cnt_s, n_near):
    lb = jnp.where(cnt_s[0, 0] == 0, 1, 0)
    return lb, jnp.where(cnt_s[lb, 0] == 0, n_near, 0), jnp.int32(0)


def near_finish(near_out, nacc):
    for lb in range(2):
        for g in range(4):
            p, gx, gy, gz, q3, xx, yy, xy, xz, yz = [nacc[lb, g, i] for i in range(10)]
            final = [p, gx, gy, gz, q3 - 3.0 * xx, q3 - 3.0 * yy, -3.0 * xy, -3.0 * xz, -3.0 * yz]
            for c in range(9):
                near_out[c, 8 * g : 8 * g + 8, lb * 128 : lb * 128 + 128] = final[c]


def near_kernel(near_ref, pos_ref, ext_ref, near_out, keys_s, picked, own_s, nacc, cnt_s):
    n_near = picked.shape[1] - 1
    total = near_setup(near_ref, pos_ref, ext_ref, keys_s, picked, own_s, nacc, cnt_s)
    first = near_first(cnt_s, n_near)
    lax.fori_loop(0, total, lambda _, st: near_item(st, picked, own_s, nacc, cnt_s), first)
    near_finish(near_out, nacc)


def near(near_rows, pos, ext):
    n_near = near_rows.shape[0]
    near_pad = jnp.pad(near_rows, ((0, 32 - n_near), (0, 0)), constant_values=-1)
    ext_pad = jnp.pad(ext, ((0, 0), (0, 0), (0, -ext.shape[2] % 128))).reshape(5 * 32, -1)
    V = pltpu.VMEM
    vm = pl.BlockSpec(memory_space=V)
    return pl.pallas_call(
        near_kernel,
        out_shape=jax.ShapeDtypeStruct((9, 32, 256), F32),
        in_specs=[vm, vm, vm],
        out_specs=vm,
        scratch_shapes=[
            V((2, 32, 128), jnp.int32),
            V((2, n_near + 1, 128, 128), F32),
            V((2, 96, 128), F32),
            V((2, 4, 10, 8, 128), F32),
            pltpu.SMEM((2, n_near + 1), jnp.int32),
        ],
        compiler_params=pltpu.CompilerParams(vmem_limit_bytes=12 * 1024 * 1024),
        cost_estimate=pl.CostEstimate(flops=250_000_000, bytes_accessed=40_000_000, transcendentals=7_000_000),
    )(near_pad, pos.reshape(96, 256), ext_pad)


def fields_inner(
    idx_ref, ops_ref, own_ref, inc_ref, out_ref, idx_s, pool, ptmp, xs, t_s, g_s, acc, *ra
):
    n_off, leaves = idx_ref.shape
    coef = ops_ref.shape[0]
    n_pad = idx_s.shape[0]
    full = n_off // 16
    ra = [ra[:NB], ra[NB:]]
    idx_s[...] = jnp.full_like(idx_s, -1)
    idx_s[0:n_off, :] = idx_ref[...]
    ptmp[...] = jnp.zeros_like(ptmp)
    for h in range(5):
        if h == 0:
            ptmp[0:coef, :] = own_ref[...].astype(F32)
        else:
            ptmp[0:coef, :] = inc_ref[(h - 1) * 256 : h * 256, :].astype(F32).T
        for c in range(8):
            pool[c, h * 16 : (h + 1) * 16, :] = ptmp[c * 16 : (c + 1) * 16, :].astype(BF)
    t_s[...] = jnp.zeros_like(t_s)
    g_s[...] = jnp.zeros_like(g_s)
    acc[...] = jnp.zeros_like(acc)
    xs[...] = jnp.zeros_like(xs)
    xs[0 : coef * 16, 0:coef] = ops_ref[:, 0:16, :].astype(F32).reshape(coef * 16, coef)
    tail = n_off - full * 16
    for k in range(coef):
        xs[4096 + k * 16 : 4096 + k * 16 + tail, 0:coef] = ops_ref[k, full * 16 : n_off, :].astype(F32)
    iota = lax.broadcasted_iota(jnp.int32, (256, 256), 0).astype(F32).astype(BF)
    one = jnp.ones((256, 256), BF)
    zero = jnp.zeros((256, 256), BF)
    half = coef - 64

    def hot(o):
        row = idx_s[pl.ds(o, 1), :]
        lo = jnp.where(row >= 0, row & 255, -1).astype(F32).astype(BF)
        return jnp.where(iota == lo, one, zero)

    def relayout(b):
        c = jnp.minimum(b // 2 + 1, full - 1)
        k0 = lax.rem(b, 2) * half
        to = pl.multiple_of(lax.rem(b // 2 + 1, 2) * 2048 + k0 * 16, 16)
        part = ops_ref[pl.ds(k0, 64), pl.ds(pl.multiple_of(c * 16, 16), 16), :]
        xs[pl.ds(to, 1024), 0:coef] = part.astype(F32).reshape(1024, coef)

    def take_ops(b, w):
        c = b // 2
        slot = jnp.where(c == full, 2, lax.rem(c, 2))
        o8 = lax.rem(b, 2) * 8
        for m in range(2):
            for u in range(2):
                x = xs[pl.ds(slot * 2048 + o8 + 4 * w + 2 * m + u, 128, stride=16), :]
                t_s[w, m, 0:128, 128 * u : 128 * u + 128] = x.astype(BF).T

    def pop_dot1(m, slot, u, c, o, buf):
        r = pltpu.matmul_pop(buf)
        hi = idx_s[pl.ds(o, 1), :] >> 8
        g = r[0:16]
        for h in range(1, 5):
            g = jnp.where(hi == h, r[16 * h : 16 * h + 16], g)
        g_s[slot, m, u * 128 + c * 16 : u * 128 + (c + 1) * 16, :] = g.astype(BF)

    def pop_dot2(m, part, buf):
        acc[m, part * M : (part + 1) * M, :] += pltpu.matmul_pop(buf)

    seq = [("a", 0, c) for c in range(8)] + [("d", 0, 0), ("d", 0, 1)] + [("a", 1, c) for c in range(8)]

    def pop(m, w, item, base, buf):
        kind, u, c = item
        if kind == "a":
            pop_dot1(m, w, u, c, base + 2 * m + u, buf)
        else:
            pop_dot2(m, c, buf)

    def issue(w, s):
        kind, u, c = seq[s]
        for m in range(2):
            buf = ra[m][s % NB]
            if kind == "a":
                pltpu.matmul_acc_lhs(buf, pool[c], load_staged_rhs=0 if c == 0 else None)
            else:
                pltpu.matmul_acc_lhs(buf, t_s[1 - w, m, c * M : (c + 1) * M, :], load_staged_rhs=1 if c == 0 else None)

    n_body = n_pad // 8
    for m in range(2):
        pltpu.matmul_push_rhs(hot(2 * m), 0, m)
    for m in range(2):
        pltpu.matmul_push_rhs(zero, 1, m)
        for s in range(len(seq) - LAG, len(seq)):
            pltpu.matmul_acc_lhs(ra[m][s % NB], pool[0], load_staged_rhs=1 if s == len(seq) - LAG else None)

    def body(b, _):
        for w in range(2):
            base = b * 8 + 4 * w
            prev = jnp.maximum(base - 4, 0)
            for s in range(len(seq)):
                issue(w, s)
                if s == 0:
                    for m in range(2):
                        pltpu.matmul_push_rhs(hot(base + 2 * m + 1), 0, m)
                if s == LAG:
                    for m in range(2):
                        pltpu.matmul_push_rhs(g_s[1 - w, m], 1, m)
                if s == 10:
                    for m in range(2):
                        pltpu.matmul_push_rhs(hot(jnp.minimum(base + 4 + 2 * m, n_pad - 1)), 0, m)
                p = s - LAG
                for m in range(2):
                    if p >= 0:
                        pop(m, w, seq[p], base, ra[m][p % NB])
                    else:
                        pop(m, 1 - w, seq[p + len(seq)], prev, ra[m][(p + len(seq)) % NB])
                if s == 11:
                    take_ops(b, w)
        relayout(b)
        return 0

    lax.fori_loop(0, n_body, body, 0)
    for s in range(len(seq) - LAG, len(seq)):
        for m in range(2):
            pop(m, 1, seq[s], n_pad - 4, ra[m][s % NB])
    for m in range(2):
        pltpu.matmul_acc_lhs(ra[m][0], pool[0], load_staged_rhs=0)
    for m in range(2):
        pltpu.matmul_pop(ra[m][0])
    for m in range(2):
        pltpu.matmul_push_rhs(g_s[1, m], 1, m)
        for c in range(2):
            pltpu.matmul_acc_lhs(ra[m][c], t_s[1, m, c * M : (c + 1) * M, :], load_staged_rhs=1 if c == 0 else None)
    for m in range(2):
        for c in range(2):
            pop_dot2(m, c, ra[m][c])
    out_ref[...] = acc[0, 0:coef, :] + acc[1, 0:coef, :]


def m2l_kernel(*refs):
    accs = [pltpu.ACC(m)((M, 256), F32) for m in range(2) for _ in range(NB)]
    pl.run_scoped(functools.partial(fields_inner, *refs), *accs)


def far_kernel(local_ref, near_ref, field_ref, harm_ref, count_ref, out_ref, der):
    coef = local_ref.shape[0]
    local = local_ref[...]
    for c in range(9):
        d = jnp.dot(field_ref[c], local, precision=lax.Precision.HIGHEST, preferred_element_type=F32)
        d = d.astype(BF).astype(F32)
        for lb in range(2):
            der[lb, c * 128 : c * 128 + coef, :] = d[:, lb * 128 : lb * 128 + 128]
    for lb in range(2):
        lanes = slice(lb * 128, lb * 128 + 128)
        for a0 in range(0, 32, 16):
            start = tuple(near_ref[c, a0 + 8 * g : a0 + 8 * g + 8, lanes] for c in range(9) for g in range(2))

            def add(i, sums):
                sums = list(sums)
                for u in range(11):
                    k = i * 11 + u
                    h = harm_ref[k, a0 : a0 + 16, lanes].astype(F32)
                    for c in range(9):
                        d = der[lb, pl.ds(c * 128 + k, 1), :]
                        for g in range(2):
                            sums[2 * c + g] = sums[2 * c + g] + d * h[8 * g : 8 * g + 8]
                return tuple(sums)

            sums = lax.fori_loop(0, coef // 11, add, start)
            for g in range(2):
                atom = lax.broadcasted_iota(jnp.int32, (8, 128), 0) + (a0 + 8 * g)
                present = atom < count_ref[0:1, lanes]
                for c in range(9):
                    out_ref[c, a0 + 8 * g : a0 + 8 * g + 8, lanes] = jnp.where(present, sums[2 * c + g], 0.0)


def fields_of(idx, ops, own, inc, near_part, field_ops, harmonics, counts):
    n_off = idx.shape[0]
    coef = ops.shape[0]
    n_pad = -(-n_off // 8) * 8
    V = pltpu.VMEM
    vm = pl.BlockSpec(memory_space=V)
    local = pl.pallas_call(
        m2l_kernel,
        out_shape=jax.ShapeDtypeStruct((coef, 256), F32),
        in_specs=[vm] * 4,
        out_specs=vm,
        scratch_shapes=[
            V((n_pad, 256), jnp.int32),
            V((8, M, 256), BF),
            V((128, 256), F32),
            V((3 * 2048, 128), F32),
            V((2, 2, 2 * M, 256), BF),
            V((2, 2, 256, 256), BF),
            V((2, 2 * M, 256), F32),
        ],
        compiler_params=pltpu.CompilerParams(vmem_limit_bytes=24 * 1024 * 1024),
        cost_estimate=pl.CostEstimate(flops=30_000_000_000, bytes_accessed=12_000_000, transcendentals=0),
    )(idx, ops, own, inc)
    return pl.pallas_call(
        far_kernel,
        out_shape=jax.ShapeDtypeStruct((9, 32, 256), F32),
        in_specs=[vm] * 5,
        out_specs=vm,
        scratch_shapes=[V((2, 9 * 128, 128), F32)],
        compiler_params=pltpu.CompilerParams(vmem_limit_bytes=24 * 1024 * 1024),
        cost_estimate=pl.CostEstimate(flops=500_000_000, bytes_accessed=5_000_000, transcendentals=0),
    )(local, near_part, field_ops, harmonics, counts)


def shards(
    multipoles,
    harmonics,
    positions,
    atom_counts,
    source_ops,
    field_ops,
    m2l_ops,
    send_list,
    m2l_list,
    near_list,
):
    axes = ("grp", "dev")
    atoms, leaves = positions.shape[1:]
    slot_ids = lax.broadcasted_iota(jnp.int32, (atoms, leaves), 0)
    present = slot_ids < atom_counts[None, :]
    masked = jnp.where(present[None], multipoles, jnp.zeros_like(multipoles))
    counts = jnp.broadcast_to(atom_counts.astype(F32)[None, None, :], (1, atoms, leaves))
    own_src = jnp.concatenate([positions, masked[0:1].astype(F32), counts], axis=0)
    extended = padded(own_src, axes, HALO)
    sources = jnp.einsum("cal,kal->ckl", masked, harmonics, preferred_element_type=F32)
    moments = jnp.einsum("ckj,ckl->jl", source_ops, sources, precision=lax.Precision.HIGHEST).astype(BF)
    coef_count = moments.shape[0]
    send_rows = send_list[0]
    slot_count = send_rows.shape[1]
    peer_count = lax.axis_size(axes)
    flat_rows = send_rows.reshape(-1)
    outgoing = jnp.take(moments, jnp.clip(flat_rows, 0, None), axis=1)
    outgoing = jnp.where(flat_rows[None, :] >= 0, outgoing, jnp.zeros_like(outgoing))
    outgoing = outgoing.T.reshape(peer_count, slot_count, coef_count)
    outgoing, extended = lax.optimization_barrier((outgoing, extended))
    arrived = lax.all_to_all(outgoing, axes, split_axis=0, concat_axis=0, tiled=True)
    incoming = arrived.reshape(peer_count * slot_count, coef_count)
    near_part = near(near_list, positions, extended)
    return fields_of(
        m2l_list, m2l_ops.transpose(1, 0, 2), moments, incoming, near_part, field_ops, harmonics, atom_counts.reshape(1, leaves)
    )


def solution(mesh):
    placed = (
        P(None, None, ("grp", "dev")),
        P(None, None, ("grp", "dev")),
        P(None, None, ("grp", "dev")),
        P(("grp", "dev")),
        P(),
        P(),
        P(),
        P(("grp", "dev"), None, None),
        P(None, ("grp", "dev")),
        P(None, ("grp", "dev")),
    )
    inner = jax.shard_map(
        shards, mesh=mesh, in_specs=placed, out_specs=P(None, None, ("grp", "dev")), check_vma=False
    )

    def whole(*args):
        with jax.sharding.use_abstract_mesh(mesh.abstract_mesh):
            return inner(*args)

    return whole
```

time: 148 us -> 126 us (0.85)
  blocking collectives: 12.4 us -> 0 us
  local copies, waits for them, and re-layouts: 18.3 us -> 15 us
  matrix products: 7.34 us -> 4.21 us
  waiting for transfers between devices: 2.67 us -> 0.01 us
  Pallas kernels: 80.9 us -> 78.4 us
  starting transfers between devices: 21 us -> 23.4 us
    all_to_all x1 -> x0, blocking collectives: 12.4 us -> none  [shards(): lax.all_to_all(sectioned, 'grp', split_axis=0, concat_axis=0, tiled=True)]
    ppermute x1, starting transfers between devices: 6.82 us -> 11.1 us  [padded(): after = lax.ppermute(value[:, :, :width], axes, down)]
    dot_general x2 -> x0, matrix products: 3.81 us -> none  [the longest x1 2.53 us: shards(): jnp.einsum('ckl,kal->cal', derived, harmonics, preferred_element_type=F32)]
    ppermute x1, waiting for transfers between devices: 2.66 us -> 0.01 us  [padded(): before = lax.ppermute(value[:, :, length - width:], axes, up)]
    pallas_call x2 -> x3, Pallas kernels: 80.9 us -> 78.4 us  [the longest x1 39.2 us: fields_of(): pl.pallas_call(m2l_kernel, out_shape=jax.ShapeDtypeStruct((coef, 256), F3...]
    dot_general x1 -> x0, local copies, waits for them, and re-layouts: 2.12 us -> none  [shards(): jnp.einsum('ckl,kal->cal', derived, harmonics, preferred_element_type=F32)]
    all_to_all x2 -> x0, local copies, waits for them, and re-layouts: 1.84 us -> none  [the longest x1 1.04 us: shards(): lax.all_to_all(lax.all_to_all(sectioned, 'grp', split_axis=0, concat_axis...]
    unnamed x15 -> x19, local copies, waits for them, and re-layouts: 8.15 us -> 8.81 us
  transfers between devices with their start and end apart: 3 -> 3, of which waited for: 1 -> 0; matrix products, arithmetic and copies ran while one was open for 0% -> 12% of each run, Pallas kernels for 27% -> 28%
where the time goes in v2:
time: 126 us
  Pallas kernels  78.4 us (62%)
  starting transfers between devices  23.4 us (19%)
  local copies, waits for them, and re-layouts  15 us (12%)
  other arithmetic  4.57 us (4%)
  matrix products  4.21 us (3%)
    pallas_call x1, Pallas kernels, fields_of(): pl.pallas_call(m2l_kernel, out_shape=jax.ShapeDtypeStruct((coef, 256), F3...  39.2 us
    pallas_call x1, Pallas kernels, near(): pl.pallas_call(near_kernel, out_shape=jax.ShapeDtypeStruct((9, 32, 256),...  34.6 us
    ppermute x1, starting transfers between devices, padded(): after = lax.ppermute(value[:, :, :width], axes, down)  11.1 us
    all_to_all x1, starting transfers between devices, shards(): lax.all_to_all(outgoing, axes, split_axis=0, concat_axis=0, tiled=True)  10.4 us
    unnamed x19, local copies, waits for them, and re-layouts  8.81 us
    pallas_call x1, Pallas kernels, fields_of(): pl.pallas_call(far_kernel, out_shape=jax.ShapeDtypeStruct((9, 32, 256), F...  4.55 us
    gather x1, local copies, waits for them, and re-layouts, shards(): outgoing = jnp.take(moments, jnp.clip(flat_rows, 0, None), axis=1)  3.21 us
    dot_general x1, matrix products, shards(): jnp.einsum('cal,kal->ckl', masked, harmonics, preferred_element_type=F32)  2.59 us
  transfers between devices with their start and end apart: 3, of which 0 were waited for; matrix products, arithmetic and copies ran while one was open for 12% of the time, Pallas kernels for 28%

profile of v2, /device:TPU:1, one launch (start us, length us, event | category | flops | bytes accessed | tf_op | source)
XLA Modules:
  0.0 125.7 jit_solution(17290234702240527623)
XLA Ops:
  0.0 0.0 copy-start
  0.0 0.0 copy-start.8
  0.0 0.0 copy-start.1
  0.0 0.8 iota_compare_fusion
  0.9 0.7 convert_element_type.16
  1.5 0.9 broadcast_select_fusion
  2.5 0.9 pad_maximum_fusion.1
  3.4 0.1 fusion.12
  3.5 11.1 %collective-permute-start.1 = (f32[5,32,16]{2,1,0:T(8,128)S(1)}, f32[5,32,16]{2,1,0:T(8,128)S(1)}, u32[]{:S(2)}, u32[]{:S(2)}) collective-permute-start(f32[5,32,16]{2,1,0:T(8,128)S(1)} %get-tuple-element.10), channel_id=1, source_target_pairs={{1,0},{2,1},{3,2},{4,3},{5,4},{6,5},{7,6},{8,7},{9,8},{10,9},{11,1... | collective-permute-start | bytes 30728 | tf_op jit(solution)/shard_map/ppermute | solution.py:18
  14.6 1.9 %collective-permute-start = (f32[5,32,16]{2,1,0:T(8,128)S(1)}, f32[5,32,16]{2,1,0:T(8,128)S(1)}, u32[]{:S(2)}, u32[]{:S(2)}) collective-permute-start(f32[5,32,16]{2,1,0:T(8,128)S(1)} %get-tuple-element.9), channel_id=1, source_target_pairs={{0,1},{1,2},{2,3},{3,4},{4,5},{5,6},{6,7},{7,8},{8,9},{9,10},{10,1... | collective-permute-start | bytes 30728 | tf_op jit(solution)/shard_map/ppermute | solution.py:17
  16.5 1.9 %copy.18 = bf16[9,32,256]{1,0,2:T(8,128)(2,1)} copy(bf16[9,32,256]{2,1,0:T(8,128)(2,1)S(1)} %broadcast_select_fusion) | data formatting | bytes 294912 | tf_op jit(solution)/shard_map/jit(_where)/select_n | solution.py:394
  18.3 0.0 copy-done.8
  18.4 0.0 copy-done.1
  18.4 4.0 %copy.19 = bf16[121,32,256]{0,1,2:T(8,128)(2,1)} copy(bf16[121,32,256]{2,1,0:T(8,128)(2,1)S(1)} %copy-done.1) | data formatting | bytes 3964928 | tf_op args[1]
  22.4 2.6 %fusion.13 = f32[256,9,121]{2,1,0:T(8,128)S(1)} fusion(bf16[9,32,256]{1,0,2:T(8,128)(2,1)} %copy.18, bf16[121,32,256]{0,1,2:T(8,128)(2,1)} %copy.19), kind=kOutput, calls=%fused_computation.18 | convolution fusion | flops 17842176 | bytes 3245056 | tf_op jit(solution)/shard_map/cal,kal->ckl/dot_general | solution.py:398
  25.0 0.0 copy-done
  25.0 1.6 %fusion.9.refs_2_ = bf16[121,256]{1,0:T(8,128)(2,1)S(1)} fusion(f32[9,121,121]{2,1,0:T(8,128)S(1)} %copy-done, f32[256,9,121]{2,1,0:T(8,128)S(1)} %fusion.13), kind=kOutput, calls=%fused_computation.6 | convolution fusion | flops 404825344 | bytes 1704164 | tf_op jit(solution)/shard_map/ckj,ckl->jl/dot_general | solution.py:399
  26.6 0.0 copy-start.3
  26.6 0.1 copy.17
  26.7 0.1 copy.16
  26.9 0.1 reshape.72
  27.0 0.0 copy-start.7
  27.0 0.2 copy.14
  27.2 0.1 ge.23
  27.3 0.2 copy.15
  27.5 0.1 le.16
  27.7 3.2 %gather_fusion = bf16[1024,121]{1,0:T(8,128)(2,1)S(1)} fusion(bf16[121,256]{0,1:T(8,128)(2,1)S(1)} %copy.17, s32[1024]{0:T(1024)S(1)} %broadcast_clamp_fusion), kind=kCustom, calls=%fused_computation | custom fusion | bytes 499712 | tf_op jit(solution)/shard_map/jit(_take)/gather | solution.py:405
  30.9 1.0 select_select_fusion
  31.9 0.0 collective-permute-done.1
  31.9 0.0 collective-permute-done
  31.9 0.0 copy-done.3
  31.9 0.2 pad_maximum_fusion
  32.1 10.4 %all-to-all-start = ((bf16[256,4,121]{2,1,0:T(4,128)(2,1)}), bf16[256,4,121]{2,1,0:T(4,128)(2,1)S(1)}, u32[]{:S(2)}, u32[]{:S(2)}) async-start(bf16[256,4,121]{2,1,0:T(4,128)(2,1)} %bitcast.4), calls=%async_computation | async-start | bytes 524288 | tf_op jit(solution)/shard_map/all_to_all | solution.py:409
  42.4 0.0 copy-done.7
  42.5 34.6 %shard_map.101.near_ref = f32[9,32,256]{2,1,0:T(8,128)S(1)} custom-call(s32[32,256]{1,0:T(8,128)S(1)} %pad.8.near_ref, f32[96,256]{1,0:T(8,128)S(1)} %bitcast.26, f32[160,384]{1,0:T(8,128)S(1)} %bitcast.28), custom_call_target="tpu_custom_call" | custom-call | flops 250000000 | bytes 40000000 | tf_op jit(solution)/shard_map/pallas_call | solution.py:157
  77.1 0.0 all-to-all-done
  77.1 0.0 copy-start.5
  77.1 3.8 %copy-done.5 = bf16[316,121,121]{2,0,1:T(8,128)(2,1)S(1)} copy-done((bf16[316,121,121]{2,0,1:T(8,128)(2,1)S(1)}, bf16[316,121,121]{2,0,1:T(8,128)(2,1)}, u32[]{:S(2)}) %copy-start.5) | copy-done | bytes 9253136
  81.0 0.0 copy-start.6
  81.0 1.0 copy-done.6
  81.9 0.0 copy-start.2
  81.9 0.0 copy-start.4
  81.9 39.2 %shard_map.100.local_ref = f32[121,256]{1,0:T(8,128)S(1)} custom-call(s32[316,256]{1,0:T(8,128)S(1)} %copy-done.6, bf16[121,316,121]{2,1,0:T(8,128)(2,1)S(1)} %bitcast.30, bf16[121,256]{1,0:T(8,128)(2,1)S(1)} %fusion.9.refs_2_, bf16[1024,121]{1,0:T(8,128)(2,1)S(1)} %bitcast.27), custom_call_target="tpu_custom_call" | custom-call | flops 30000001024 | bytes 12000000 | tf_op jit(solution)/shard_map/pallas_call | solution.py:350
  121.1 0.0 copy-done.2
  121.1 0.0 copy-done.4
  121.2 4.6 %shard_map.102 = f32[9,32,256]{2,1,0:T(8,128)} custom-call(f32[121,256]{1,0:T(8,128)S(1)} %shard_map.100.local_ref, f32[9,32,256]{2,1,0:T(8,128)S(1)} %shard_map.101.near_ref, f32[9,121,121]{2,1,0:T(8,128)S(1)} %copy-done.2, bf16[121,32,256]{2,1,0:T(8,128)(2,1)S(1)} %copy-done.1, s32[1,256]{1,0:T(1,128)S(1)} %bitcast.29), custom_call_target="tpu_custom_call" | custom-call | flops 500000000 | bytes 5000000 | tf_op jit(solution)/shard_map/pallas_call | solution.py:367
  (7 shorter events, 0.0 us)
Async XLA Ops:
  0.0 25.0 %copy-start = (f32[9,121,121]{2,1,0:T(8,128)S(1)}, f32[9,121,121]{2,1,0:T(8,128)}, u32[]{:S(2)}) copy-start(f32[9,121,121]{2,1,0:T(8,128)} %param.14) | copy-start | bytes 1581232
  0.0 18.3 %copy-start.8 = (s32[1,256,4]{1,2,0:T(4,128)S(1)}, s32[1,256,4]{1,2,0:T(4,128)}, u32[]{:S(2)}) copy-start(s32[1,256,4]{1,2,0:T(4,128)} %param.17) | copy-start | bytes 12292
  0.0 18.3 %copy-start.1 = (bf16[121,32,256]{2,1,0:T(8,128)(2,1)S(1)}, bf16[121,32,256]{2,1,0:T(8,128)(2,1)}, u32[]{:S(2)}) copy-start(bf16[121,32,256]{2,1,0:T(8,128)(2,1)} %harm_ref.1) | copy-start | bytes 5947396
  3.5 28.4 %collective-permute-start.1 = (f32[5,32,16]{2,1,0:T(8,128)S(1)}, f32[5,32,16]{2,1,0:T(8,128)S(1)}, u32[]{:S(2)}, u32[]{:S(2)}) collective-permute-start(f32[5,32,16]{2,1,0:T(8,128)S(1)} %get-tuple-element.10), channel_id=1, source_target_pairs={{1,0},{2,1},{3,2},{4,3},{5,4},{6,5},{7,6},{8,7},{9,8},{10,9},{11,1... | collective-permute-start | bytes 30728 | tf_op jit(solution)/shard_map/ppermute | solution.py:18
  14.6 17.4 %collective-permute-start = (f32[5,32,16]{2,1,0:T(8,128)S(1)}, f32[5,32,16]{2,1,0:T(8,128)S(1)}, u32[]{:S(2)}, u32[]{:S(2)}) collective-permute-start(f32[5,32,16]{2,1,0:T(8,128)S(1)} %get-tuple-element.9), channel_id=1, source_target_pairs={{0,1},{1,2},{2,3},{3,4},{4,5},{5,6},{6,7},{7,8},{8,9},{9,10},{10,1... | collective-permute-start | bytes 30728 | tf_op jit(solution)/shard_map/ppermute | solution.py:17
  26.6 5.3 %copy-start.3 = (f32[3,32,256]{2,1,0:T(8,128)S(1)}, f32[3,32,256]{2,1,0:T(8,128)}, u32[]{:S(2)}) copy-start(f32[3,32,256]{2,1,0:T(8,128)} %param.12) | copy-start | bytes 294916
  27.0 15.5 %copy-start.7 = (s32[27,256]{1,0:T(8,128)S(1)}, s32[27,256]{1,0:T(8,128)}, u32[]{:S(2)}) copy-start(s32[27,256]{1,0:T(8,128)} %param.19) | copy-start | bytes 82948
  32.1 45.0 %all-to-all-start = ((bf16[256,4,121]{2,1,0:T(4,128)(2,1)}), bf16[256,4,121]{2,1,0:T(4,128)(2,1)S(1)}, u32[]{:S(2)}, u32[]{:S(2)}) async-start(bf16[256,4,121]{2,1,0:T(4,128)(2,1)} %bitcast.4), calls=%async_computation | async-start | bytes 524288 | tf_op jit(solution)/shard_map/all_to_all | solution.py:409
  77.1 3.8 %copy-start.5 = (bf16[316,121,121]{2,0,1:T(8,128)(2,1)S(1)}, bf16[316,121,121]{2,0,1:T(8,128)(2,1)}, u32[]{:S(2)}) copy-start(bf16[316,121,121]{2,0,1:T(8,128)(2,1)} %param.16) | copy-start | bytes 27759340
  81.0 1.0 copy-start.6
  81.9 39.2 %copy-start.2 = (f32[9,121,121]{2,1,0:T(8,128)S(1)}, f32[9,121,121]{2,1,0:T(8,128)}, u32[]{:S(2)}) copy-start(f32[9,121,121]{2,1,0:T(8,128)} %field_ref.1) | copy-start | bytes 1581232
  81.9 39.2 %copy-start.4 = (s32[256]{0:T(256)S(1)}, s32[256]{0:T(256)}, u32[]{:S(2)}) copy-start(s32[256]{0:T(256)} %param.13) | copy-start | bytes 3076

commit v3 on v2

--- a/solution.py
+++ b/solution.py
@@ -375,6 +375,63 @@
     )(local, near_part, field_ops, harmonics, counts)
 
 
+def moments_kernel(mult_ref, harm_ref, count_ref, ops_ref, send_ref, mom_ref, out_ref, src, rows_s):
+    comps, atoms, _ = mult_ref.shape
+    coef = harm_ref.shape[0]
+    src[...] = jnp.zeros_like(src)
+    for lb in range(2):
+        lanes = slice(lb * 128, lb * 128 + 128)
+        held = []
+        for c in range(comps):
+            for g in range(atoms // 16):
+                atom = lax.broadcasted_iota(jnp.int32, (16, 128), 0) + 16 * g
+                value = mult_ref[c, 16 * g : 16 * g + 16, lanes].astype(F32)
+                held.append(jnp.where(atom < count_ref[0:1, lanes], value, 0.0))
+
+        def add(i, held):
+            for u in range(11):
+                k = i * 11 + u
+                h = harm_ref[k, :, lanes].astype(F32)
+                for c in range(comps):
+                    part = held[2 * c] * h[0:16] + held[2 * c + 1] * h[16:32]
+                    src[lb, pl.ds(c * 128 + k, 1), :] = jnp.sum(part[0:8] + part[8:16], axis=0, keepdims=True)
+            return held
+
+        lax.fori_loop(0, coef // 11, add, tuple(held))
+    mom = jnp.zeros((coef, 256), F32)
+    for c in range(comps):
+        s = jnp.concatenate([src[lb, c * 128 : c * 128 + coef, :] for lb in range(2)], axis=1)
+        mom += lax.dot_general(
+            ops_ref[c], s, (((0,), (0,)), ((), ())), precision=lax.Precision.HIGHEST, preferred_element_type=F32
+        )
+    mom = mom.astype(BF)
+    mom_ref[...] = mom
+    leaf = lax.broadcasted_iota(jnp.int32, (256, 256), 0)
+    slots = send_ref.shape[0]
+    rows_s[...] = jnp.zeros_like(rows_s)
+    for i in range(slots):
+        hot = jnp.where(leaf == send_ref[i : i + 1, :], 1.0, 0.0).astype(BF)
+        picked = jnp.dot(mom, hot, preferred_element_type=F32)
+        rows_s[pl.ds(i, 256, stride=slots), 0:128] = jnp.pad(picked, ((0, 128 - coef), (0, 0))).T
+    out_ref[...] = rows_s[:, 0:coef].astype(BF)
+
+
+def moments_of(multipoles, harmonics, counts, source_ops, send_rows):
+    coef = harmonics.shape[0]
+    V = pltpu.VMEM
+    vm = pl.BlockSpec(memory_space=V)
+    peers = send_rows.shape[1] * send_rows.shape[0]
+    return pl.pallas_call(
+        moments_kernel,
+        out_shape=(jax.ShapeDtypeStruct((coef, 256), BF), jax.ShapeDtypeStruct((peers, coef), BF)),
+        in_specs=[vm] * 5,
+        out_specs=(vm, vm),
+        scratch_shapes=[V((2, 9 * 128, 128), F32), V((peers, 128), F32)],
+        compiler_params=pltpu.CompilerParams(vmem_limit_bytes=16 * 1024 * 1024),
+        cost_estimate=pl.CostEstimate(flops=500_000_000, bytes_accessed=5_000_000, transcendentals=0),
+    )(multipoles, harmonics, counts, source_ops, send_rows)
+
+
 def shards(
     multipoles,
     harmonics,
@@ -395,22 +452,17 @@
     counts = jnp.broadcast_to(atom_counts.astype(F32)[None, None, :], (1, atoms, leaves))
     own_src = jnp.concatenate([positions, masked[0:1].astype(F32), counts], axis=0)
     extended = padded(own_src, axes, HALO)
-    sources = jnp.einsum("cal,kal->ckl", masked, harmonics, preferred_element_type=F32)
-    moments = jnp.einsum("ckj,ckl->jl", source_ops, sources, precision=lax.Precision.HIGHEST).astype(BF)
+    counts_row = atom_counts.reshape(1, leaves)
+    moments, outgoing = moments_of(multipoles, harmonics, counts_row, source_ops, send_list[0].T)
+    peer_count, slot_count = send_list.shape[1:]
     coef_count = moments.shape[0]
-    send_rows = send_list[0]
-    slot_count = send_rows.shape[1]
-    peer_count = lax.axis_size(axes)
-    flat_rows = send_rows.reshape(-1)
-    outgoing = jnp.take(moments, jnp.clip(flat_rows, 0, None), axis=1)
-    outgoing = jnp.where(flat_rows[None, :] >= 0, outgoing, jnp.zeros_like(outgoing))
-    outgoing = outgoing.T.reshape(peer_count, slot_count, coef_count)
+    outgoing = outgoing.reshape(peer_count, slot_count, coef_count)
     outgoing, extended = lax.optimization_barrier((outgoing, extended))
     arrived = lax.all_to_all(outgoing, axes, split_axis=0, concat_axis=0, tiled=True)
     incoming = arrived.reshape(peer_count * slot_count, coef_count)
     near_part = near(near_list, positions, extended)
     return fields_of(
-        m2l_list, m2l_ops.transpose(1, 0, 2), moments, incoming, near_part, field_ops, harmonics, atom_counts.reshape(1, leaves)
+        m2l_list, m2l_ops.transpose(1, 0, 2), moments, incoming, near_part, field_ops, harmonics, counts_row
     )
 
 

time: 126 us -> 124 us (0.984); the launches traced: 126 us -> 122 us
  Pallas kernels: 78.4 us -> 83.9 us
  local copies, waits for them, and re-layouts: 15 us -> 10.5 us
  matrix products: 4.21 us -> 0 us
    pallas_call x0 -> x1, Pallas kernels: none -> 6.38 us  [moments_of(): pl.pallas_call(moments_kernel, out_shape=(jax.ShapeDtypeStruct((coef, 256...]
    dot_general x2 -> x0, matrix products: 4.21 us -> none  [the longest x1 2.59 us: shards(): jnp.einsum('cal,kal->ckl', masked, harmonics, preferred_element_type=F32)]
    gather x1 -> x0, local copies, waits for them, and re-layouts: 3.21 us -> none  [shards(): outgoing = jnp.take(moments, jnp.clip(flat_rows, 0, None), axis=1)]
    select_n x2 -> x0, other arithmetic: 1.97 us -> none  [the longest x1 1.04 us: shards(): jnp.where(flat_rows[None, :] >= 0, outgoing, jnp.zeros_like(outgoing))]
    select_n x1 -> x0, local copies, waits for them, and re-layouts: 1.85 us -> none  [shards(): masked = jnp.where(present[None], multipoles, jnp.zeros_like(multipoles))]
    unnamed x19 -> x22, local copies, waits for them, and re-layouts: 8.81 us -> 9.6 us
  transfers between devices with their start and end apart: 3 -> 3, of which waited for: 0 -> 0; matrix products, arithmetic and copies ran while one was open for 12% -> 1% of each run, Pallas kernels for 28% -> 33%
where the time goes in v3:
time: 124 us; the launch traced here: 122 us
  Pallas kernels  83.9 us (68%)
  starting transfers between devices  23.4 us (19%)
  local copies, waits for them, and re-layouts  10.5 us (8%)
  other arithmetic  4.09 us (3%)
    pallas_call x1, Pallas kernels, fields_of(): pl.pallas_call(m2l_kernel, out_shape=jax.ShapeDtypeStruct((coef, 256), F3...  39.2 us
    pallas_call x1, Pallas kernels, near(): pl.pallas_call(near_kernel, out_shape=jax.ShapeDtypeStruct((9, 32, 256),...  33.8 us
    ppermute x1, starting transfers between devices, padded(): after = lax.ppermute(value[:, :, :width], axes, down)  11.1 us
    all_to_all x1, starting transfers between devices, shards(): lax.all_to_all(outgoing, axes, split_axis=0, concat_axis=0, tiled=True)  10.4 us
    unnamed x22, local copies, waits for them, and re-layouts  9.6 us
    pallas_call x1, Pallas kernels, moments_of(): pl.pallas_call(moments_kernel, out_shape=(jax.ShapeDtypeStruct((coef, 256...  6.38 us
    pallas_call x1, Pallas kernels, fields_of(): pl.pallas_call(far_kernel, out_shape=jax.ShapeDtypeStruct((9, 32, 256), F...  4.56 us
  transfers between devices with their start and end apart: 3, of which 0 were waited for; matrix products, arithmetic and copies ran while one was open for 1% of the time, Pallas kernels for 33%

profile of v3, /device:TPU:1, one launch (start us, length us, event | category | flops | bytes accessed | tf_op | source)
XLA Modules:
  0.0 122.0 jit_solution(9346886488219026443)
XLA Ops:
  0.0 0.0 copy-start.10
  0.0 0.7 convert_element_type.9
  0.7 0.7 iota_compare_fusion
  1.4 0.7 fusion
  2.1 0.9 pad_maximum_fusion.1
  3.1 0.1 fusion.1
  3.1 11.1 %collective-permute-start.1 = (f32[5,32,16]{2,1,0:T(8,128)S(1)}, f32[5,32,16]{2,1,0:T(8,128)S(1)}, u32[]{:S(2)}, u32[]{:S(2)}) collective-permute-start(f32[5,32,16]{2,1,0:T(8,128)S(1)} %get-tuple-element.14), channel_id=1, source_target_pairs={{1,0},{2,1},{3,2},{4,3},{5,4},{6,5},{7,6},{8,7},{9,8},{10,9},{11,1... | collective-permute-start | bytes 30728 | tf_op jit(solution)/shard_map/ppermute | solution.py:18
  14.2 1.9 %collective-permute-start = (f32[5,32,16]{2,1,0:T(8,128)S(1)}, f32[5,32,16]{2,1,0:T(8,128)S(1)}, u32[]{:S(2)}, u32[]{:S(2)}) collective-permute-start(f32[5,32,16]{2,1,0:T(8,128)S(1)} %get-tuple-element.13), channel_id=1, source_target_pairs={{0,1},{1,2},{2,3},{3,4},{4,5},{5,6},{6,7},{7,8},{8,9},{9,10},{10,1... | collective-permute-start | bytes 30728 | tf_op jit(solution)/shard_map/ppermute | solution.py:17
  16.2 0.0 copy-start
  16.2 1.5 %copy-done = bf16[121,32,256]{2,1,0:T(8,128)(2,1)S(1)} copy-done((bf16[121,32,256]{2,1,0:T(8,128)(2,1)S(1)}, bf16[121,32,256]{2,1,0:T(8,128)(2,1)}, u32[]{:S(2)}) %copy-start) | copy-done | bytes 1982488
  17.7 0.0 copy-start.2
  17.7 1.1 copy-done.2
  18.8 0.0 copy-start.5
  18.8 0.9 copy-done.5
  19.7 0.0 copy-start.6
  19.7 0.7 copy-done.6
  20.4 0.0 copy-start.8
  20.4 0.7 copy-done.8
  21.0 6.4 %shard_map.100 = (bf16[121,256]{1,0:T(8,128)(2,1)S(1)}, bf16[1024,121]{1,0:T(8,128)(2,1)}) custom-call(bf16[9,32,256]{2,1,0:T(8,128)(2,1)S(1)} %copy-done.5, bf16[121,32,256]{2,1,0:T(8,128)(2,1)S(1)} %copy-done, s32[1,256]{1,0:T(1,128)S(1)} %bitcast.12, f32[9,121,121]{2,1,0:T(8,128)S(1)} %copy-done.2, s32[4,256]{1,0:T(4,128)S(1)} %bitcast.14), custom_call_target="tpu_custom_call" | custom-call | flops 500000000 | bytes 5000000 | tf_op jit(solution)/shard_map/pallas_call | solution.py:424
  27.4 0.0 collective-permute-done.1
  27.4 0.0 collective-permute-done
  27.4 1.0 pad_maximum_fusion
  28.5 10.4 %all-to-all-start = ((bf16[256,4,121]{2,1,0:T(4,128)(2,1)}), bf16[256,4,121]{2,1,0:T(4,128)(2,1)S(1)}, u32[]{:S(2)}, u32[]{:S(2)}) async-start(bf16[256,4,121]{2,1,0:T(4,128)(2,1)} %bitcast.4), calls=%async_computation | async-start | bytes 524288 | tf_op jit(solution)/shard_map/all_to_all | solution.py:461
  38.9 0.8 pad.8.near_ref
  39.6 0.0 copy-start.4
  39.7 0.9 copy-done.4
  40.5 33.8 %shard_map.102.near_ref = f32[9,32,256]{2,1,0:T(8,128)S(1)} custom-call(s32[32,256]{1,0:T(8,128)S(1)} %pad.8.near_ref, f32[96,256]{1,0:T(8,128)S(1)} %bitcast.9, f32[160,384]{1,0:T(8,128)S(1)} %bitcast.11), custom_call_target="tpu_custom_call" | custom-call | flops 250000000 | bytes 40000000 | tf_op jit(solution)/shard_map/pallas_call | solution.py:157
  74.3 0.0 all-to-all-done
  74.3 0.0 copy-done.10
  74.4 0.0 copy-start.9
  74.4 3.8 %copy-done.9 = bf16[316,121,121]{2,0,1:T(8,128)(2,1)S(1)} copy-done((bf16[316,121,121]{2,0,1:T(8,128)(2,1)S(1)}, bf16[316,121,121]{2,0,1:T(8,128)(2,1)}, u32[]{:S(2)}) %copy-start.9) | copy-done | bytes 9253136
  78.2 0.0 copy-start.1
  78.2 0.0 copy-start.3
  78.2 0.0 copy-start.7
  78.2 39.2 %shard_map.101.local_ref = f32[121,256]{1,0:T(8,128)S(1)} custom-call(s32[316,256]{1,0:T(8,128)S(1)} %copy-done.10, bf16[121,316,121]{2,1,0:T(8,128)(2,1)S(1)} %bitcast.15, bf16[121,256]{1,0:T(8,128)(2,1)S(1)} %get-tuple-element.9.refs_2_, bf16[1024,121]{1,0:T(8,128)(2,1)S(1)} %bitcast.10), custom_call_target="tpu_custom_call" | custom-call | flops 30000001024 | bytes 12000000 | tf_op jit(solution)/shard_map/pallas_call | solution.py:350
  117.4 0.0 copy-done.1
  117.4 0.0 copy-done.3
  117.4 0.0 copy-done.7
  117.4 4.6 %shard_map.103 = f32[9,32,256]{2,1,0:T(8,128)} custom-call(f32[121,256]{1,0:T(8,128)S(1)} %shard_map.101.local_ref, f32[9,32,256]{2,1,0:T(8,128)S(1)} %shard_map.102.near_ref, f32[9,121,121]{2,1,0:T(8,128)S(1)} %copy-done.3, bf16[121,32,256]{2,1,0:T(8,128)(2,1)S(1)} %copy-done.1, s32[1,256]{1,0:T(1,128)S(1)} %bitcast.13), custom_call_target="tpu_custom_call" | custom-call | flops 500000000 | bytes 5000000 | tf_op jit(solution)/shard_map/pallas_call | solution.py:367
  (2 shorter events, 0.0 us)
Async XLA Ops:
  0.0 74.3 %copy-start.10 = (s32[316,256]{1,0:T(8,128)S(1)}, s32[316,256]{1,0:T(8,128)}, u32[]{:S(2)}) copy-start(s32[316,256]{1,0:T(8,128)} %refs_0_.1) | copy-start | bytes 970756
  3.1 24.3 %collective-permute-start.1 = (f32[5,32,16]{2,1,0:T(8,128)S(1)}, f32[5,32,16]{2,1,0:T(8,128)S(1)}, u32[]{:S(2)}, u32[]{:S(2)}) collective-permute-start(f32[5,32,16]{2,1,0:T(8,128)S(1)} %get-tuple-element.14), channel_id=1, source_target_pairs={{1,0},{2,1},{3,2},{4,3},{5,4},{6,5},{7,6},{8,7},{9,8},{10,9},{11,1... | collective-permute-start | bytes 30728 | tf_op jit(solution)/shard_map/ppermute | solution.py:18
  14.2 13.2 %collective-permute-start = (f32[5,32,16]{2,1,0:T(8,128)S(1)}, f32[5,32,16]{2,1,0:T(8,128)S(1)}, u32[]{:S(2)}, u32[]{:S(2)}) collective-permute-start(f32[5,32,16]{2,1,0:T(8,128)S(1)} %get-tuple-element.13), channel_id=1, source_target_pairs={{0,1},{1,2},{2,3},{3,4},{4,5},{5,6},{6,7},{7,8},{8,9},{9,10},{10,1... | collective-permute-start | bytes 30728 | tf_op jit(solution)/shard_map/ppermute | solution.py:17
  16.2 1.6 %copy-start = (bf16[121,32,256]{2,1,0:T(8,128)(2,1)S(1)}, bf16[121,32,256]{2,1,0:T(8,128)(2,1)}, u32[]{:S(2)}) copy-start(bf16[121,32,256]{2,1,0:T(8,128)(2,1)} %harm_ref.3) | copy-start | bytes 5947396
  17.7 1.1 copy-start.2
  18.8 0.9 copy-start.5
  19.7 0.7 copy-start.6
  20.4 0.7 copy-start.8
  28.5 45.9 %all-to-all-start = ((bf16[256,4,121]{2,1,0:T(4,128)(2,1)}), bf16[256,4,121]{2,1,0:T(4,128)(2,1)S(1)}, u32[]{:S(2)}, u32[]{:S(2)}) async-start(bf16[256,4,121]{2,1,0:T(4,128)(2,1)} %bitcast.4), calls=%async_computation | async-start | bytes 524288 | tf_op jit(solution)/shard_map/all_to_all | solution.py:461
  39.6 0.9 copy-start.4
  74.4 3.8 %copy-start.9 = (bf16[316,121,121]{2,0,1:T(8,128)(2,1)S(1)}, bf16[316,121,121]{2,0,1:T(8,128)(2,1)}, u32[]{:S(2)}) copy-start(bf16[316,121,121]{2,0,1:T(8,128)(2,1)} %param.16) | copy-start | bytes 27759340
  78.2 39.2 %copy-start.1 = (bf16[121,32,256]{2,1,0:T(8,128)(2,1)S(1)}, bf16[121,32,256]{2,1,0:T(8,128)(2,1)}, u32[]{:S(2)}) copy-start(bf16[121,32,256]{2,1,0:T(8,128)(2,1)} %harm_ref.3) | copy-start | bytes 5947396
  78.2 39.2 %copy-start.3 = (f32[9,121,121]{2,1,0:T(8,128)S(1)}, f32[9,121,121]{2,1,0:T(8,128)}, u32[]{:S(2)}) copy-start(f32[9,121,121]{2,1,0:T(8,128)} %field_ref.1) | copy-start | bytes 1581232
  78.2 39.2 %copy-start.7 = (s32[256]{0:T(256)S(1)}, s32[256]{0:T(256)}, u32[]{:S(2)}) copy-start(s32[256]{0:T(256)} %param.13) | copy-start | bytes 3076

commit v4 on v3

--- a/solution.py
+++ b/solution.py
@@ -10,13 +10,14 @@
 F32 = jnp.float32
 BF = jnp.bfloat16
 HALO = 16
-def padded(value, axes, width):
-    count, length = (lax.axis_size(axes), value.shape[2])
-    up = [(i, (i + 1) % count) for i in range(count - 1)]
+def halos(first, last, axes):
+    count = lax.axis_size(axes)
+    up = [(i, i + 1) for i in range(count - 1)]
     down = [(j, i) for i, j in up]
-    before = lax.ppermute(value[:, :, length - width :], axes, up)
-    after = lax.ppermute(value[:, :, :width], axes, down)
-    return jnp.concatenate([before, value, after], axis=2)
+    empty = jnp.zeros_like(first)
+    before = lax.ppermute(jnp.concatenate([last, empty], axis=2), axes, up)
+    after = lax.ppermute(jnp.concatenate([empty, first], axis=2), axes, down)
+    return before, after
 
 
 NB, LAG, M = 6, 5, 80
@@ -48,17 +49,32 @@
     return value
 
 
-def near_setup(near_ref, own_ref, ext_ref, keys_s, picked, own_s, nacc, cnt_s):
+def near_setup(rows_ref, pos_ref, mult_ref, count_ref, before_ref, after_ref, near_ref, ext_ref, keys_s, picked, own_s, nacc, cnt_s):
+    atoms, leaves = pos_ref.shape[1:]
+    width = before_ref.shape[2] // 2
+    near_ref[...] = jnp.full_like(near_ref, -1)
+    near_ref[0 : rows_ref.shape[0], :] = rows_ref[...]
+    ext_ref[...] = jnp.zeros_like(ext_ref)
+    for c in range(3):
+        ext_ref[32 * c : 32 * c + 32, 0:leaves] = pos_ref[c]
+    atom = lax.broadcasted_iota(jnp.int32, (atoms, leaves), 0)
+    charge = jnp.where(atom < count_ref[...], mult_ref[...].astype(F32), 0.0)
+    ext_ref[96:128, 0:leaves] = charge
+    ext_ref[128:136, 0:leaves] = jnp.broadcast_to(count_ref[...].astype(F32), (8, leaves))
+    for c in range(4):
+        ext_ref[32 * c : 32 * c + 32, leaves : leaves + 2 * width] = before_ref[c] + after_ref[c]
+    ext_ref[128:136, leaves : leaves + 2 * width] = before_ref[4, 0:8] + after_ref[4, 0:8]
     blocks = ext_ref.shape[1] // 128
     n_near = picked.shape[1] - 1
     nacc[...] = jnp.zeros_like(nacc)
     for lb in range(2):
         lanes = slice(lb * 128, lb * 128 + 128)
-        own_s[lb] = own_ref[:, lanes]
+        own_s[lb] = ext_ref[0:96, lanes]
         picked[lb, n_near] = jnp.zeros((128, 128), F32)
         for r in range(0, 32, 8):
             pos = near_ref[r : r + 8, lanes]
             safe = jnp.maximum(pos, 0)
+            safe = jnp.where(safe < width, safe + leaves, jnp.where(safe < leaves + width, safe - width, safe))
             count = take_lanes(ext_ref, 128, safe & 127, safe >> 7, blocks)
             keys_s[lb, r : r + 8, :] = jnp.where(pos >= 0, count.astype(jnp.int32) * 512 + safe, 0)
     ks = [keys_s[:, r, :] for r in range(32)]
@@ -140,26 +156,31 @@
                 near_out[c, 8 * g : 8 * g + 8, lb * 128 : lb * 128 + 128] = final[c]
 
 
-def near_kernel(near_ref, pos_ref, ext_ref, near_out, keys_s, picked, own_s, nacc, cnt_s):
+def near_kernel(
+    rows_ref, pos_ref, mult_ref, count_ref, before_ref, after_ref, near_out,
+    near_s, ext_s, keys_s, picked, own_s, nacc, cnt_s
+):
     n_near = picked.shape[1] - 1
-    total = near_setup(near_ref, pos_ref, ext_ref, keys_s, picked, own_s, nacc, cnt_s)
+    total = near_setup(
+        rows_ref, pos_ref, mult_ref, count_ref, before_ref, after_ref, near_s, ext_s, keys_s, picked, own_s, nacc, cnt_s
+    )
     first = near_first(cnt_s, n_near)
     lax.fori_loop(0, total, lambda _, st: near_item(st, picked, own_s, nacc, cnt_s), first)
     near_finish(near_out, nacc)
 
 
-def near(near_rows, pos, ext):
+def near(near_rows, pos, charges, counts, before, after):
     n_near = near_rows.shape[0]
-    near_pad = jnp.pad(near_rows, ((0, 32 - n_near), (0, 0)), constant_values=-1)
-    ext_pad = jnp.pad(ext, ((0, 0), (0, 0), (0, -ext.shape[2] % 128))).reshape(5 * 32, -1)
     V = pltpu.VMEM
     vm = pl.BlockSpec(memory_space=V)
     return pl.pallas_call(
         near_kernel,
         out_shape=jax.ShapeDtypeStruct((9, 32, 256), F32),
-        in_specs=[vm, vm, vm],
+        in_specs=[vm] * 6,
         out_specs=vm,
         scratch_shapes=[
+            V((32, 256), jnp.int32),
+            V((136, 384), F32),
             V((2, 32, 128), jnp.int32),
             V((2, n_near + 1, 128, 128), F32),
             V((2, 96, 128), F32),
@@ -168,7 +189,7 @@
         ],
         compiler_params=pltpu.CompilerParams(vmem_limit_bytes=12 * 1024 * 1024),
         cost_estimate=pl.CostEstimate(flops=250_000_000, bytes_accessed=40_000_000, transcendentals=7_000_000),
-    )(near_pad, pos.reshape(96, 256), ext_pad)
+    )(near_rows, pos, charges, counts, before, after)
 
 
 def fields_inner(
@@ -427,7 +448,7 @@
         in_specs=[vm] * 5,
         out_specs=(vm, vm),
         scratch_shapes=[V((2, 9 * 128, 128), F32), V((peers, 128), F32)],
-        compiler_params=pltpu.CompilerParams(vmem_limit_bytes=16 * 1024 * 1024),
+        compiler_params=pltpu.CompilerParams(vmem_limit_bytes=58 * 1024 * 1024),
         cost_estimate=pl.CostEstimate(flops=500_000_000, bytes_accessed=5_000_000, transcendentals=0),
     )(multipoles, harmonics, counts, source_ops, send_rows)
 
@@ -446,21 +467,23 @@
 ):
     axes = ("grp", "dev")
     atoms, leaves = positions.shape[1:]
-    slot_ids = lax.broadcasted_iota(jnp.int32, (atoms, leaves), 0)
-    present = slot_ids < atom_counts[None, :]
-    masked = jnp.where(present[None], multipoles, jnp.zeros_like(multipoles))
-    counts = jnp.broadcast_to(atom_counts.astype(F32)[None, None, :], (1, atoms, leaves))
-    own_src = jnp.concatenate([positions, masked[0:1].astype(F32), counts], axis=0)
-    extended = padded(own_src, axes, HALO)
+    def ends(cut):
+        count = atom_counts[cut][None, :]
+        slot = lax.broadcasted_iota(jnp.int32, (atoms, HALO), 0)
+        charge = jnp.where(slot < count, multipoles[0, :, cut].astype(F32), 0.0)
+        filled = jnp.broadcast_to(count.astype(F32), (atoms, HALO))
+        return jnp.concatenate([positions[:, :, cut], charge[None], filled[None]], axis=0)
+
+    before, after = halos(ends(slice(0, HALO)), ends(slice(leaves - HALO, leaves)), axes)
     counts_row = atom_counts.reshape(1, leaves)
     moments, outgoing = moments_of(multipoles, harmonics, counts_row, source_ops, send_list[0].T)
     peer_count, slot_count = send_list.shape[1:]
     coef_count = moments.shape[0]
     outgoing = outgoing.reshape(peer_count, slot_count, coef_count)
-    outgoing, extended = lax.optimization_barrier((outgoing, extended))
+    outgoing, before, after = lax.optimization_barrier((outgoing, before, after))
     arrived = lax.all_to_all(outgoing, axes, split_axis=0, concat_axis=0, tiled=True)
     incoming = arrived.reshape(peer_count * slot_count, coef_count)
-    near_part = near(near_list, positions, extended)
+    near_part = near(near_list, positions, multipoles[0], counts_row, before, after)
     return fields_of(
         m2l_list, m2l_ops.transpose(1, 0, 2), moments, incoming, near_part, field_ops, harmonics, counts_row
     )

time: 124 us -> 119 us (0.960); the launches traced: 122 us -> 118 us
  local copies, waits for them, and re-layouts: 10.5 us -> 7.78 us
  Pallas kernels: 83.9 us -> 86.4 us
  other arithmetic: 4.09 us -> 1.72 us
    unnamed x22 -> x18, local copies, waits for them, and re-layouts: 9.6 us -> 6.16 us
    concatenate x2, other arithmetic: 1.95 us -> 0.1 us  [ends(): jnp.concatenate([positions[:, :, cut], charge[None], filled[None]], axis=0)]
    pallas_call x1, Pallas kernels: 6.38 us -> 8.06 us  [moments_of(): pl.pallas_call(moments_kernel, out_shape=(jax.ShapeDtypeStruct((coef, 256...]
    convert_element_type x2 -> x0, other arithmetic: 1.45 us -> none  [the longest x1 0.73 us: shards(): atom_counts.astype(F32)[None, None, :]]
  transfers between devices with their start and end apart: 3 -> 3, of which waited for: 0 -> 0; matrix products, arithmetic and copies ran while one was open for 1% -> 1% of each run, Pallas kernels for 33% -> 36%
where the time goes in v4:
time: 119 us; the launch traced here: 118 us
  Pallas kernels  86.4 us (73%)
  starting transfers between devices  22.4 us (19%)
  local copies, waits for them, and re-layouts  7.78 us (7%)
  other arithmetic  1.72 us (1%)
    pallas_call x1, Pallas kernels, fields_of(): pl.pallas_call(m2l_kernel, out_shape=jax.ShapeDtypeStruct((coef, 256), F3...  39.2 us
    pallas_call x1, Pallas kernels, near(): pl.pallas_call(near_kernel, out_shape=jax.ShapeDtypeStruct((9, 32, 256),...  34.6 us
    all_to_all x1, starting transfers between devices, shards(): lax.all_to_all(outgoing, axes, split_axis=0, concat_axis=0, tiled=True)  9.37 us
    ppermute x1, starting transfers between devices, halos(): after = lax.ppermute(jnp.concatenate([empty, first], axis=2), axes, down)  9.04 us
    pallas_call x1, Pallas kernels, moments_of(): pl.pallas_call(moments_kernel, out_shape=(jax.ShapeDtypeStruct((coef, 256...  8.06 us
    unnamed x18, local copies, waits for them, and re-layouts  6.16 us
    pallas_call x1, Pallas kernels, fields_of(): pl.pallas_call(far_kernel, out_shape=jax.ShapeDtypeStruct((9, 32, 256), F...  4.56 us
    ppermute x1, starting transfers between devices, halos(): before = lax.ppermute(jnp.concatenate([last, empty], axis=2), axes, up)  3.95 us
  transfers between devices with their start and end apart: 3, of which 0 were waited for; matrix products, arithmetic and copies ran while one was open for 1% of the time, Pallas kernels for 36%

profile of v4, /device:TPU:1, one launch (start us, length us, event | category | flops | bytes accessed | tf_op | source)
XLA Modules:
  0.0 118.4 jit_solution(16944867095530713551)
XLA Ops:
  0.0 0.0 copy-start.6
  0.0 0.8 fusion.1
  0.8 0.9 fusion
  1.7 0.8 convert_select_fusion
  2.5 3.9 %collective-permute-start = (f32[5,32,32]{2,1,0:T(8,128)S(1)}, f32[5,32,32]{2,1,0:T(8,128)S(1)}, u32[]{:S(2)}, u32[]{:S(2)}) collective-permute-start(f32[5,32,32]{2,1,0:T(8,128)S(1)} %select_maximum_fusion.2), channel_id=1, source_target_pairs={{0,1},{1,2},{2,3},{3,4},{4,5},{5,6},{6,7},{7,8},{8,9},{9,10},{10,1... | collective-permute-start | bytes 61448 | tf_op jit(solution)/shard_map/ppermute | solution.py:18
  6.5 0.1 select_maximum_fusion
  6.6 9.0 %collective-permute-start.1 = (f32[5,32,32]{2,1,0:T(8,128)S(1)}, f32[5,32,32]{2,1,0:T(8,128)S(1)}, u32[]{:S(2)}, u32[]{:S(2)}) collective-permute-start(f32[5,32,32]{2,1,0:T(8,128)S(1)} %select_maximum_fusion), channel_id=1, source_target_pairs={{1,0},{2,1},{3,2},{4,3},{5,4},{6,5},{7,6},{8,7},{9,8},{10,9},{11,1... | collective-permute-start | bytes 61448 | tf_op jit(solution)/shard_map/ppermute | solution.py:19
  15.7 8.1 %shard_map.100 = (bf16[121,256]{1,0:T(8,128)(2,1)}, bf16[1024,121]{1,0:T(8,128)(2,1)}) custom-call(bf16[9,32,256]{2,1,0:T(8,128)(2,1)} %mult_ref.1, bf16[121,32,256]{2,1,0:T(8,128)(2,1)} %harm_ref.3, s32[1,256]{1,0:T(1,128)} %bitcast.10, f32[9,121,121]{2,1,0:T(8,128)} %ops_ref.1, s32[4,256]{1,0:T(4,128)} %bitcast.15), custom_call_target="tpu_custom_call" | custom-call | flops 500000000 | bytes 5000000 | tf_op jit(solution)/shard_map/pallas_call | solution.py:445
  23.7 0.0 copy-start.7
  23.7 0.0 collective-permute-done.before_ref
  23.7 0.0 collective-permute-done.1.after_ref
  23.7 9.4 %all-to-all-start = ((bf16[256,4,121]{2,1,0:T(4,128)(2,1)}), bf16[256,4,121]{2,1,0:T(4,128)(2,1)S(1)}, u32[]{:S(2)}, u32[]{:S(2)}) async-start(bf16[256,4,121]{2,1,0:T(4,128)(2,1)} %bitcast.14), calls=%async_computation | async-start | bytes 524288 | tf_op jit(solution)/shard_map/all_to_all | solution.py:484
  33.1 0.7 slice_bitcast_fusion.mult_ref
  33.8 0.0 copy-start.2
  33.8 0.9 copy-done.2
  34.7 0.0 copy-start.3
  34.7 0.7 copy-done.3
  35.4 0.0 copy-start.8
  35.4 0.8 copy-done.8
  36.2 34.6 %shard_map.102.near_ref = f32[9,32,256]{2,1,0:T(8,128)S(1)} custom-call(s32[27,256]{1,0:T(8,128)S(1)} %copy-done.8, f32[3,32,256]{2,1,0:T(8,128)S(1)} %copy-done.2, bf16[32,256]{1,0:T(8,128)(2,1)S(1)} %slice_bitcast_fusion.mult_ref, s32[1,256]{1,0:T(1,128)S(1)} %bitcast.11, f32[5,32,32]{2,1,0:T(8,128)S(1)} %collective-permute-done.before_ref, ...), custom_call_target="tpu_custom_call" | custom-call | flops 250000000 | bytes 40000000 | tf_op jit(solution)/shard_map/pallas_call | solution.py:176
  70.7 0.0 all-to-all-done
  70.7 0.0 copy-done.6
  70.8 0.0 copy-done.7
  70.8 0.0 copy-start.5
  70.8 3.8 %copy-done.5 = bf16[316,121,121]{2,0,1:T(8,128)(2,1)S(1)} copy-done((bf16[316,121,121]{2,0,1:T(8,128)(2,1)S(1)}, bf16[316,121,121]{2,0,1:T(8,128)(2,1)}, u32[]{:S(2)}) %copy-start.5) | copy-done | bytes 9253136
  74.6 0.0 copy-start
  74.6 0.0 copy-start.1
  74.6 0.0 copy-start.4
  74.6 39.2 %shard_map.101.local_ref = f32[121,256]{1,0:T(8,128)S(1)} custom-call(s32[316,256]{1,0:T(8,128)S(1)} %copy-done.6, bf16[121,316,121]{2,1,0:T(8,128)(2,1)S(1)} %bitcast.13, bf16[121,256]{1,0:T(8,128)(2,1)S(1)} %copy-done.7, bf16[1024,121]{1,0:T(8,128)(2,1)S(1)} %bitcast.9), custom_call_target="tpu_custom_call" | custom-call | flops 30000001024 | bytes 12000000 | tf_op jit(solution)/shard_map/pallas_call | solution.py:371
  113.8 0.0 copy-done
  113.8 0.0 copy-done.1
  113.8 0.0 copy-done.4
  113.8 4.6 %shard_map.103 = f32[9,32,256]{2,1,0:T(8,128)} custom-call(f32[121,256]{1,0:T(8,128)S(1)} %shard_map.101.local_ref, f32[9,32,256]{2,1,0:T(8,128)S(1)} %shard_map.102.near_ref, f32[9,121,121]{2,1,0:T(8,128)S(1)} %copy-done.1, bf16[121,32,256]{2,1,0:T(8,128)(2,1)S(1)} %copy-done, s32[1,256]{1,0:T(1,128)S(1)} %bitcast.12), custom_call_target="tpu_custom_call" | custom-call | flops 500000000 | bytes 5000000 | tf_op jit(solution)/shard_map/pallas_call | solution.py:388
  (3 shorter events, 0.0 us)
Async XLA Ops:
  0.0 70.7 %copy-start.6 = (s32[316,256]{1,0:T(8,128)S(1)}, s32[316,256]{1,0:T(8,128)}, u32[]{:S(2)}) copy-start(s32[316,256]{1,0:T(8,128)} %refs_0_.1) | copy-start | bytes 970756
  2.5 21.2 %collective-permute-start = (f32[5,32,32]{2,1,0:T(8,128)S(1)}, f32[5,32,32]{2,1,0:T(8,128)S(1)}, u32[]{:S(2)}, u32[]{:S(2)}) collective-permute-start(f32[5,32,32]{2,1,0:T(8,128)S(1)} %select_maximum_fusion.2), channel_id=1, source_target_pairs={{0,1},{1,2},{2,3},{3,4},{4,5},{5,6},{6,7},{7,8},{8,9},{9,10},{10,1... | collective-permute-start | bytes 61448 | tf_op jit(solution)/shard_map/ppermute | solution.py:18
  6.6 17.1 %collective-permute-start.1 = (f32[5,32,32]{2,1,0:T(8,128)S(1)}, f32[5,32,32]{2,1,0:T(8,128)S(1)}, u32[]{:S(2)}, u32[]{:S(2)}) collective-permute-start(f32[5,32,32]{2,1,0:T(8,128)S(1)} %select_maximum_fusion), channel_id=1, source_target_pairs={{1,0},{2,1},{3,2},{4,3},{5,4},{6,5},{7,6},{8,7},{9,8},{10,9},{11,1... | collective-permute-start | bytes 61448 | tf_op jit(solution)/shard_map/ppermute | solution.py:19
  23.7 47.0 %copy-start.7 = (bf16[121,256]{1,0:T(8,128)(2,1)S(1)}, bf16[121,256]{1,0:T(8,128)(2,1)}, u32[]{:S(2)}) copy-start(bf16[121,256]{1,0:T(8,128)(2,1)} %get-tuple-element.10.refs_2_) | copy-start | bytes 185860
  23.7 47.0 %all-to-all-start = ((bf16[256,4,121]{2,1,0:T(4,128)(2,1)}), bf16[256,4,121]{2,1,0:T(4,128)(2,1)S(1)}, u32[]{:S(2)}, u32[]{:S(2)}) async-start(bf16[256,4,121]{2,1,0:T(4,128)(2,1)} %bitcast.14), calls=%async_computation | async-start | bytes 524288 | tf_op jit(solution)/shard_map/all_to_all | solution.py:484
  33.8 0.9 copy-start.2
  34.7 0.7 copy-start.3
  35.4 0.8 copy-start.8
  70.8 3.8 %copy-start.5 = (bf16[316,121,121]{2,0,1:T(8,128)(2,1)S(1)}, bf16[316,121,121]{2,0,1:T(8,128)(2,1)}, u32[]{:S(2)}) copy-start(bf16[316,121,121]{2,0,1:T(8,128)(2,1)} %param.16) | copy-start | bytes 27759340
  74.6 39.2 %copy-start = (bf16[121,32,256]{2,1,0:T(8,128)(2,1)S(1)}, bf16[121,32,256]{2,1,0:T(8,128)(2,1)}, u32[]{:S(2)}) copy-start(bf16[121,32,256]{2,1,0:T(8,128)(2,1)} %harm_ref.3) | copy-start | bytes 5947396
  74.6 39.2 %copy-start.1 = (f32[9,121,121]{2,1,0:T(8,128)S(1)}, f32[9,121,121]{2,1,0:T(8,128)}, u32[]{:S(2)}) copy-start(f32[9,121,121]{2,1,0:T(8,128)} %field_ref.1) | copy-start | bytes 1581232
  74.6 39.2 %copy-start.4 = (s32[256]{0:T(256)S(1)}, s32[256]{0:T(256)}, u32[]{:S(2)}) copy-start(s32[256]{0:T(256)} %param.13) | copy-start | bytes 3076

commit v5 on v4

--- a/solution.py
+++ b/solution.py
@@ -58,7 +58,7 @@
     for c in range(3):
         ext_ref[32 * c : 32 * c + 32, 0:leaves] = pos_ref[c]
     atom = lax.broadcasted_iota(jnp.int32, (atoms, leaves), 0)
-    charge = jnp.where(atom < count_ref[...], mult_ref[...].astype(F32), 0.0)
+    charge = jnp.where(atom < count_ref[...], mult_ref[0].astype(F32), 0.0)
     ext_ref[96:128, 0:leaves] = charge
     ext_ref[128:136, 0:leaves] = jnp.broadcast_to(count_ref[...].astype(F32), (8, leaves))
     for c in range(4):
@@ -169,7 +169,7 @@
     near_finish(near_out, nacc)
 
 
-def near(near_rows, pos, charges, counts, before, after):
+def near(near_rows, pos, multipoles, counts, before, after):
     n_near = near_rows.shape[0]
     V = pltpu.VMEM
     vm = pl.BlockSpec(memory_space=V)
@@ -187,9 +187,9 @@
             V((2, 4, 10, 8, 128), F32),
             pltpu.SMEM((2, n_near + 1), jnp.int32),
         ],
-        compiler_params=pltpu.CompilerParams(vmem_limit_bytes=12 * 1024 * 1024),
+        compiler_params=pltpu.CompilerParams(vmem_limit_bytes=58 * 1024 * 1024),
         cost_estimate=pl.CostEstimate(flops=250_000_000, bytes_accessed=40_000_000, transcendentals=7_000_000),
-    )(near_rows, pos, charges, counts, before, after)
+    )(near_rows, pos, multipoles, counts, before, after)
 
 
 def fields_inner(
@@ -483,7 +483,7 @@
     outgoing, before, after = lax.optimization_barrier((outgoing, before, after))
     arrived = lax.all_to_all(outgoing, axes, split_axis=0, concat_axis=0, tiled=True)
     incoming = arrived.reshape(peer_count * slot_count, coef_count)
-    near_part = near(near_list, positions, multipoles[0], counts_row, before, after)
+    near_part = near(near_list, positions, multipoles, counts_row, before, after)
     return fields_of(
         m2l_list, m2l_ops.transpose(1, 0, 2), moments, incoming, near_part, field_ops, harmonics, counts_row
     )

time: 119 us -> 118 us (level)
  local copies, waits for them, and re-layouts: 7.78 us -> 4.74 us
  Pallas kernels: 86.4 us -> 88.3 us
    unnamed x18, local copies, waits for them, and re-layouts: 6.16 us -> 3.84 us
    pallas_call x1, Pallas kernels: 34.6 us -> 36.4 us  [near(): pl.pallas_call(near_kernel, out_shape=jax.ShapeDtypeStruct((9, 32, 256),...]
  transfers between devices with their start and end apart: 3 -> 3, of which waited for: 0 -> 0; matrix products, arithmetic and copies ran while one was open for 1% -> 0% of each run, Pallas kernels for 36% -> 38%
where the time goes in v5:
time: 118 us; the launch traced here: 117 us
  Pallas kernels  88.3 us (75%)
  starting transfers between devices  22.4 us (19%)
  local copies, waits for them, and re-layouts  4.74 us (4%)
  other arithmetic  1.72 us (1%)
    pallas_call x1, Pallas kernels, fields_of(): pl.pallas_call(m2l_kernel, out_shape=jax.ShapeDtypeStruct((coef, 256), F3...  39.2 us
    pallas_call x1, Pallas kernels, near(): pl.pallas_call(near_kernel, out_shape=jax.ShapeDtypeStruct((9, 32, 256),...  36.4 us
    all_to_all x1, starting transfers between devices, shards(): lax.all_to_all(outgoing, axes, split_axis=0, concat_axis=0, tiled=True)  9.38 us
    ppermute x1, starting transfers between devices, halos(): after = lax.ppermute(jnp.concatenate([empty, first], axis=2), axes, down)  9.04 us
    pallas_call x1, Pallas kernels, moments_of(): pl.pallas_call(moments_kernel, out_shape=(jax.ShapeDtypeStruct((coef, 256...  8.06 us
    pallas_call x1, Pallas kernels, fields_of(): pl.pallas_call(far_kernel, out_shape=jax.ShapeDtypeStruct((9, 32, 256), F...  4.56 us
    ppermute x1, starting transfers between devices, halos(): before = lax.ppermute(jnp.concatenate([last, empty], axis=2), axes, up)  3.95 us
    unnamed x18, local copies, waits for them, and re-layouts  3.84 us
  transfers between devices with their start and end apart: 3, of which 0 were waited for; matrix products, arithmetic and copies ran while one was open for 0% of the time, Pallas kernels for 38%

profile of v5, /device:TPU:1, one launch (start us, length us, event | category | flops | bytes accessed | tf_op | source)
XLA Modules:
  0.0 117.2 jit_solution(9444462765601497060)
XLA Ops:
  0.0 0.0 copy-start.5
  0.0 0.8 fusion.1
  0.8 0.9 fusion
  1.7 0.8 convert_select_fusion
  2.5 3.9 %collective-permute-start = (f32[5,32,32]{2,1,0:T(8,128)S(1)}, f32[5,32,32]{2,1,0:T(8,128)S(1)}, u32[]{:S(2)}, u32[]{:S(2)}) collective-permute-start(f32[5,32,32]{2,1,0:T(8,128)S(1)} %select_maximum_fusion.2), channel_id=1, source_target_pairs={{0,1},{1,2},{2,3},{3,4},{4,5},{5,6},{6,7},{7,8},{8,9},{9,10},{10,1... | collective-permute-start | bytes 61448 | tf_op jit(solution)/shard_map/ppermute | solution.py:18
  6.5 0.1 select_maximum_fusion
  6.6 9.0 %collective-permute-start.1 = (f32[5,32,32]{2,1,0:T(8,128)S(1)}, f32[5,32,32]{2,1,0:T(8,128)S(1)}, u32[]{:S(2)}, u32[]{:S(2)}) collective-permute-start(f32[5,32,32]{2,1,0:T(8,128)S(1)} %select_maximum_fusion), channel_id=1, source_target_pairs={{1,0},{2,1},{3,2},{4,3},{5,4},{6,5},{7,6},{8,7},{9,8},{10,9},{11,1... | collective-permute-start | bytes 61448 | tf_op jit(solution)/shard_map/ppermute | solution.py:19
  15.7 8.1 %shard_map.100 = (bf16[121,256]{1,0:T(8,128)(2,1)}, bf16[1024,121]{1,0:T(8,128)(2,1)}) custom-call(bf16[9,32,256]{2,1,0:T(8,128)(2,1)} %mult_ref.3, bf16[121,32,256]{2,1,0:T(8,128)(2,1)} %harm_ref.3, s32[1,256]{1,0:T(1,128)} %bitcast.8, f32[9,121,121]{2,1,0:T(8,128)} %ops_ref.1, s32[4,256]{1,0:T(4,128)} %bitcast.13), custom_call_target="tpu_custom_call" | custom-call | flops 500000000 | bytes 5000000 | tf_op jit(solution)/shard_map/pallas_call | solution.py:445
  23.7 0.0 copy-start.6
  23.7 0.0 collective-permute-done.before_ref
  23.7 0.0 copy-start.7
  23.7 0.0 collective-permute-done.1.after_ref
  23.7 0.0 copy-start.8
  23.7 9.4 %all-to-all-start = ((bf16[256,4,121]{2,1,0:T(4,128)(2,1)}), bf16[256,4,121]{2,1,0:T(4,128)(2,1)S(1)}, u32[]{:S(2)}, u32[]{:S(2)}) async-start(bf16[256,4,121]{2,1,0:T(4,128)(2,1)} %bitcast.12), calls=%async_computation | async-start | bytes 524288 | tf_op jit(solution)/shard_map/all_to_all | solution.py:484
  33.1 0.0 copy-done.7
  33.1 0.0 copy-done.8
  33.1 36.4 %shard_map.102.near_ref = f32[9,32,256]{2,1,0:T(8,128)} custom-call(s32[27,256]{1,0:T(8,128)} %rows_ref.1, f32[3,32,256]{2,1,0:T(8,128)} %pos_ref.1, bf16[9,32,256]{2,1,0:T(8,128)(2,1)} %mult_ref.3, s32[1,256]{1,0:T(1,128)} %bitcast.9, f32[5,32,32]{2,1,0:T(8,128)} %copy-done.7, f32[5,32,32]{2,1,0:T(8,128)} %copy-done.8), custom_call_target="tpu_custom_call" | custom-call | flops 250000000 | bytes 40000000 | tf_op jit(solution)/shard_map/pallas_call | solution.py:176
  69.6 0.0 all-to-all-done
  69.6 0.0 copy-done.5
  69.6 0.0 copy-done.6
  69.6 0.0 copy-start.4
  69.6 3.8 %copy-done.4 = bf16[316,121,121]{2,0,1:T(8,128)(2,1)S(1)} copy-done((bf16[316,121,121]{2,0,1:T(8,128)(2,1)S(1)}, bf16[316,121,121]{2,0,1:T(8,128)(2,1)}, u32[]{:S(2)}) %copy-start.4) | copy-done | bytes 9253136
  73.4 0.0 copy-start
  73.4 0.0 copy-start.1
  73.4 0.0 copy-start.2
  73.4 0.0 copy-start.3
  73.4 39.2 %shard_map.101.local_ref = f32[121,256]{1,0:T(8,128)S(1)} custom-call(s32[316,256]{1,0:T(8,128)S(1)} %copy-done.5, bf16[121,316,121]{2,1,0:T(8,128)(2,1)S(1)} %bitcast.11, bf16[121,256]{1,0:T(8,128)(2,1)S(1)} %copy-done.6, bf16[1024,121]{1,0:T(8,128)(2,1)S(1)} %bitcast.7), custom_call_target="tpu_custom_call" | custom-call | flops 30000001024 | bytes 12000000 | tf_op jit(solution)/shard_map/pallas_call | solution.py:371
  112.6 0.0 copy-done
  112.6 0.0 copy-done.1
  112.7 0.0 copy-done.2
  112.7 0.0 copy-done.3
  112.7 4.6 %shard_map.103 = f32[9,32,256]{2,1,0:T(8,128)} custom-call(f32[121,256]{1,0:T(8,128)S(1)} %shard_map.101.local_ref, f32[9,32,256]{2,1,0:T(8,128)S(1)} %copy-done.2, f32[9,121,121]{2,1,0:T(8,128)S(1)} %copy-done.1, bf16[121,32,256]{2,1,0:T(8,128)(2,1)S(1)} %copy-done, s32[1,256]{1,0:T(1,128)S(1)} %bitcast.10), custom_call_target="tpu_custom_call" | custom-call | flops 500000000 | bytes 5000000 | tf_op jit(solution)/shard_map/pallas_call | solution.py:388
  (3 shorter events, 0.0 us)
Async XLA Ops:
  0.0 69.6 %copy-start.5 = (s32[316,256]{1,0:T(8,128)S(1)}, s32[316,256]{1,0:T(8,128)}, u32[]{:S(2)}) copy-start(s32[316,256]{1,0:T(8,128)} %refs_0_.1) | copy-start | bytes 970756
  2.5 21.2 %collective-permute-start = (f32[5,32,32]{2,1,0:T(8,128)S(1)}, f32[5,32,32]{2,1,0:T(8,128)S(1)}, u32[]{:S(2)}, u32[]{:S(2)}) collective-permute-start(f32[5,32,32]{2,1,0:T(8,128)S(1)} %select_maximum_fusion.2), channel_id=1, source_target_pairs={{0,1},{1,2},{2,3},{3,4},{4,5},{5,6},{6,7},{7,8},{8,9},{9,10},{10,1... | collective-permute-start | bytes 61448 | tf_op jit(solution)/shard_map/ppermute | solution.py:18
  6.6 17.1 %collective-permute-start.1 = (f32[5,32,32]{2,1,0:T(8,128)S(1)}, f32[5,32,32]{2,1,0:T(8,128)S(1)}, u32[]{:S(2)}, u32[]{:S(2)}) collective-permute-start(f32[5,32,32]{2,1,0:T(8,128)S(1)} %select_maximum_fusion), channel_id=1, source_target_pairs={{1,0},{2,1},{3,2},{4,3},{5,4},{6,5},{7,6},{8,7},{9,8},{10,9},{11,1... | collective-permute-start | bytes 61448 | tf_op jit(solution)/shard_map/ppermute | solution.py:19
  23.7 45.9 %copy-start.6 = (bf16[121,256]{1,0:T(8,128)(2,1)S(1)}, bf16[121,256]{1,0:T(8,128)(2,1)}, u32[]{:S(2)}) copy-start(bf16[121,256]{1,0:T(8,128)(2,1)} %get-tuple-element.10.refs_2_) | copy-start | bytes 185860
  23.7 9.4 %copy-start.7 = (f32[5,32,32]{2,1,0:T(8,128)}, f32[5,32,32]{2,1,0:T(8,128)S(1)}, u32[]{:S(2)}) copy-start(f32[5,32,32]{2,1,0:T(8,128)S(1)} %collective-permute-done.before_ref) | copy-start | bytes 61444
  23.7 9.4 %copy-start.8 = (f32[5,32,32]{2,1,0:T(8,128)}, f32[5,32,32]{2,1,0:T(8,128)S(1)}, u32[]{:S(2)}) copy-start(f32[5,32,32]{2,1,0:T(8,128)S(1)} %collective-permute-done.1.after_ref) | copy-start | bytes 61444
  23.7 45.9 %all-to-all-start = ((bf16[256,4,121]{2,1,0:T(4,128)(2,1)}), bf16[256,4,121]{2,1,0:T(4,128)(2,1)S(1)}, u32[]{:S(2)}, u32[]{:S(2)}) async-start(bf16[256,4,121]{2,1,0:T(4,128)(2,1)} %bitcast.12), calls=%async_computation | async-start | bytes 524288 | tf_op jit(solution)/shard_map/all_to_all | solution.py:484
  69.6 3.8 %copy-start.4 = (bf16[316,121,121]{2,0,1:T(8,128)(2,1)S(1)}, bf16[316,121,121]{2,0,1:T(8,128)(2,1)}, u32[]{:S(2)}) copy-start(bf16[316,121,121]{2,0,1:T(8,128)(2,1)} %param.16) | copy-start | bytes 27759340
  73.4 39.2 %copy-start = (bf16[121,32,256]{2,1,0:T(8,128)(2,1)S(1)}, bf16[121,32,256]{2,1,0:T(8,128)(2,1)}, u32[]{:S(2)}) copy-start(bf16[121,32,256]{2,1,0:T(8,128)(2,1)} %harm_ref.3) | copy-start | bytes 5947396
  73.4 39.2 %copy-start.1 = (f32[9,121,121]{2,1,0:T(8,128)S(1)}, f32[9,121,121]{2,1,0:T(8,128)}, u32[]{:S(2)}) copy-start(f32[9,121,121]{2,1,0:T(8,128)} %field_ref.1) | copy-start | bytes 1581232
  73.4 39.2 %copy-start.2 = (f32[9,32,256]{2,1,0:T(8,128)S(1)}, f32[9,32,256]{2,1,0:T(8,128)}, u32[]{:S(2)}) copy-start(f32[9,32,256]{2,1,0:T(8,128)} %shard_map.102.near_ref) | copy-start | bytes 884740
  73.4 39.2 %copy-start.3 = (s32[256]{0:T(256)S(1)}, s32[256]{0:T(256)}, u32[]{:S(2)}) copy-start(s32[256]{0:T(256)} %param.13) | copy-start | bytes 3076
